TPU v7x, 256 devices: a whole 4x4x8 slice. The times are simulated.
256 devices in a mesh: seq: 256 (over y, x, z, core).
Axes of the slice: x: 4, y: 4, z: 8, core: 2. Of those that a mesh axis runs over, the one named last changes fastest.
Arguments:
- signal: float32 [262144, 256], P('seq'), may hold values from -6 to 6
- conv_weight: bfloat16 [6, 768, 512], replicated, may hold values from -0.21875 to 0.21875
- conv_bias: float32 [6, 512], replicated, may hold values from -3 to 3
- res_weight: bfloat16 [6, 256, 256], replicated, may hold values from -0.375 to 0.375
- skip_weight: bfloat16 [6, 256, 256], replicated, may hold values from -0.375 to 0.375
Outputs:
- features: float32 [262144, 256], P('seq')
- skip_sum: float32 [262144, 256], P('seq')
All inputs are finite; a program needn't handle non-finite values.
Results may differ from a plain program's by a relative error of at most 0.0051.
Values may be sent and summed in bfloat16 or wider, within the bound.
A program may use at most 64 MiB of HBM per device.

v0:
```python
import jax
import jax.numpy as jnp
from jax import lax
from jax.sharding import PartitionSpec as P

LAYERS = 6


def passed_along(value, axis, steps):
    count = lax.axis_size(axis)
    leading, last = (max(0, -steps), min(count, count - steps))
    return lax.ppermute(value, axis, [(source, source + steps) for source in range(leading, last)])


def fetch_rows(rounded, shifted_rows):
    row_count = rounded.shape[0]
    if shifted_rows < row_count:
        tail_piece = passed_along(rounded[row_count - shifted_rows :], "seq", 1)
        head_piece = passed_along(rounded[:shifted_rows], "seq", -1)
        before_rows = jnp.concatenate([tail_piece, rounded[: row_count - shifted_rows]], 0)
        following_rows = jnp.concatenate([rounded[shifted_rows:], head_piece], 0)
    else:
        device_hops = shifted_rows // row_count
        before_rows = passed_along(rounded, "seq", device_hops)
        following_rows = passed_along(rounded, "seq", -device_hops)
    return (before_rows, following_rows)


def gate_layer(
    pre_gate, gated_dims, index_of_layer, conv_bias, res_weight, skip_weight, current, skip_sum
):
    pre_gate = pre_gate + conv_bias[index_of_layer]
    gated = (jnp.tanh(pre_gate[:, :gated_dims]) * jax.nn.sigmoid(pre_gate[:, gated_dims:])).astype(
        jnp.bfloat16
    )
    current = current + jnp.dot(
        gated, res_weight[index_of_layer], preferred_element_type=jnp.float32
    )
    skip_sum = skip_sum + jnp.dot(
        gated, skip_weight[index_of_layer], preferred_element_type=jnp.float32
    )
    return (current, skip_sum)


def body(signal, conv_weight, conv_bias, res_weight, skip_weight):
    row_count, channels = signal.shape
    current = signal
    skip_sum = jnp.zeros_like(signal)
    for index_of_layer in range(LAYERS):
        shifted_rows = row_count // 2 * 2**index_of_layer
        rounded = current.astype(jnp.bfloat16)
        weights = conv_weight[index_of_layer]
        before_rows, following_rows = fetch_rows(rounded, shifted_rows)
        joined_rows = jnp.concatenate([before_rows, rounded, following_rows], 1)
        pre_gate = jnp.dot(joined_rows, weights, preferred_element_type=jnp.float32)
        current, skip_sum = gate_layer(
            pre_gate,
            channels,
            index_of_layer,
            conv_bias,
            res_weight,
            skip_weight,
            current,
            skip_sum,
        )
    return (current, skip_sum)


def solution(mesh):
    in_specs = (P("seq", None), P(), P(), P(), P())
    out_specs = (P("seq", None), P("seq", None))
    return jax.shard_map(body, mesh=mesh, in_specs=in_specs, out_specs=out_specs, check_vma=False)
```

profile of v0, /device:TPU:22, one launch (start us, length us, event | category | flops | bytes accessed | tf_op | source)
XLA Modules:
  0.0 175.7 jit_solution(2038567349817964060)
XLA Ops:
  0.6 1.4 convert_element_type.36
  2.1 1.9 %collective-permute-start = (bf16[512,256]{1,0:T(8,128)(2,1)S(1)}, bf16[512,256]{1,0:T(8,128)(2,1)S(1)}, u32[]{:S(2)}, u32[]{:S(2)}) collective-permute-start(bf16[512,256]{1,0:T(8,128)(2,1)S(1)} %get-tuple-element.4), channel_id=1, source_target_pairs={{0,1},{1,2},{2,3},{3,4},{4,5},{5,6},{6,7},{7,8},{8,9},{9,10},{10,1... | collective-permute-start | bytes 786440 | tf_op jit(solution)/shard_map/ppermute | solution.py:12
  4.0 7.5 %collective-permute-start.1 = (bf16[512,256]{1,0:T(8,128)(2,1)S(1)}, bf16[512,256]{1,0:T(8,128)(2,1)}, u32[]{:S(2)}, u32[]{:S(2)}) collective-permute-start(bf16[512,256]{1,0:T(8,128)(2,1)S(1)} %get-tuple-element.5), channel_id=1, source_target_pairs={{1,0},{2,1},{3,2},{4,3},{5,4},{6,5},{7,6},{8,7},{9,8},{10,9},{11,1... | collective-permute-start | bytes 786440 | tf_op jit(solution)/shard_map/ppermute | solution.py:12
  11.8 1.7 collective-permute-done
  13.6 1.8 collective-permute-done.1
  15.3 2.2 %convolution_add_fusion.5 = f32[1024,512]{1,0:T(8,128)S(1)} fusion(bf16[512,256]{1,0:T(8,128)(2,1)} %collective-permute-done.1, bf16[512,256]{1,0:T(8,128)(2,1)S(1)} %get-tuple-element.4, bf16[1024,256]{1,0:T(8,128)(2,1)S(1)} %convert_element_type.36, bf16[512,256]{1,0:T(8,128)(2,1)S(1)} %get-tuple-element.5, bf16[512,256]{1,0:T(8,128)(2,1)S(1)} %collective-permute-done, ...), kind=kOutput, calls=%fused_computation.5 | convolution fusion | flops 813694976 | bytes 4458496 | tf_op jit(solution)/shard_map/dot_general | solution.py:55
  19.0 2.2 %collective-permute-start.2 = (bf16[1024,256]{0,1:T(8,128)(2,1)S(1)}, bf16[1024,256]{0,1:T(8,128)(2,1)S(1)}, u32[]{:S(2)}, u32[]{:S(2)}) collective-permute-start(bf16[1024,256]{0,1:T(8,128)(2,1)S(1)} %get-tuple-element.12), channel_id=1, source_target_pairs={{0,1},{1,2},{2,3},{3,4},{4,5},{5,6},{6,7},{7,8},{8,9},{9,10},{10,1... | collective-permute-start | bytes 1572872 | tf_op jit(solution)/shard_map/ppermute | solution.py:12
  21.2 6.0 %collective-permute-start.3 = (bf16[1024,256]{0,1:T(8,128)(2,1)S(1)}, bf16[1024,256]{0,1:T(8,128)(2,1)S(1)}, u32[]{:S(2)}, u32[]{:S(2)}) collective-permute-start(bf16[1024,256]{0,1:T(8,128)(2,1)S(1)} %get-tuple-element.12), channel_id=1, source_target_pairs={{1,0},{2,1},{3,2},{4,3},{5,4},{6,5},{7,6},{8,7},{9,8},{10,9},{11,1... | collective-permute-start | bytes 1572872 | tf_op jit(solution)/shard_map/ppermute | solution.py:12
  27.3 4.9 %collective-permute-done.2 = bf16[1024,256]{0,1:T(8,128)(2,1)S(1)} collective-permute-done((bf16[1024,256]{0,1:T(8,128)(2,1)S(1)}, bf16[1024,256]{0,1:T(8,128)(2,1)S(1)}, u32[]{:S(2)}, u32[]{:S(2)}) %collective-permute-start.2) | collective-permute-done | bytes 524320 | tf_op jit(solution)/shard_map/ppermute | solution.py:12
  32.2 1.8 collective-permute-done.3
  33.9 2.2 %convolution_add_fusion.4 = f32[1024,512]{1,0:T(8,128)S(1)} fusion(bf16[1024,256]{0,1:T(8,128)(2,1)S(1)} %collective-permute-done.3, bf16[1024,256]{0,1:T(8,128)(2,1)S(1)} %get-tuple-element.12, bf16[1024,256]{0,1:T(8,128)(2,1)S(1)} %collective-permute-done.2, f32[512]{0:T(512)S(1)} %bitcast.86, bf16[6,768,512]{2,1,0:T(8,128)(2,1)} %param.6), kind=kOutput, calls=%fused_computation.4 | convolution fusion | flops 810549248 | bytes 4458496 | tf_op jit(solution)/shard_map/dot_general | solution.py:55
  36.9 1.9 %collective-permute-start.4 = (bf16[1024,256]{0,1:T(8,128)(2,1)S(1)}, bf16[1024,256]{0,1:T(8,128)(2,1)S(1)}, u32[]{:S(2)}, u32[]{:S(2)}) collective-permute-start(bf16[1024,256]{0,1:T(8,128)(2,1)S(1)} %get-tuple-element.14), channel_id=1, source_target_pairs={{0,2},{1,3},{2,4},{3,5},{4,6},{5,7},{6,8},{7,9},{8,10},{9,11},{10,... | collective-permute-start | bytes 1572872 | tf_op jit(solution)/shard_map/ppermute | solution.py:12
  38.9 6.0 %collective-permute-start.5 = (bf16[1024,256]{0,1:T(8,128)(2,1)S(1)}, bf16[1024,256]{0,1:T(8,128)(2,1)S(1)}, u32[]{:S(2)}, u32[]{:S(2)}) collective-permute-start(bf16[1024,256]{0,1:T(8,128)(2,1)S(1)} %get-tuple-element.14), channel_id=1, source_target_pairs={{2,0},{3,1},{4,2},{5,3},{6,4},{7,5},{8,6},{9,7},{10,8},{11,9},{12,... | collective-permute-start | bytes 1572872 | tf_op jit(solution)/shard_map/ppermute | solution.py:12
  44.9 10.4 %collective-permute-done.4 = bf16[1024,256]{0,1:T(8,128)(2,1)S(1)} collective-permute-done((bf16[1024,256]{0,1:T(8,128)(2,1)S(1)}, bf16[1024,256]{0,1:T(8,128)(2,1)S(1)}, u32[]{:S(2)}, u32[]{:S(2)}) %collective-permute-start.4) | collective-permute-done | bytes 524320 | tf_op jit(solution)/shard_map/ppermute | solution.py:12
  55.3 1.2 collective-permute-done.5
  56.5 1.0 convolution_add_fusion.3
  58.3 2.7 %collective-permute-start.6 = (bf16[1024,256]{0,1:T(8,128)(2,1)S(1)}, bf16[1024,256]{0,1:T(8,128)(2,1)S(1)}, u32[]{:S(2)}, u32[]{:S(2)}) collective-permute-start(bf16[1024,256]{0,1:T(8,128)(2,1)S(1)} %get-tuple-element.16), channel_id=1, source_target_pairs={{0,4},{1,5},{2,6},{3,7},{4,8},{5,9},{6,10},{7,11},{8,12},{9,13},{1... | collective-permute-start | bytes 1572872 | tf_op jit(solution)/shard_map/ppermute | solution.py:12
  61.0 6.2 %collective-permute-start.7 = (bf16[1024,256]{0,1:T(8,128)(2,1)S(1)}, bf16[1024,256]{0,1:T(8,128)(2,1)S(1)}, u32[]{:S(2)}, u32[]{:S(2)}) collective-permute-start(bf16[1024,256]{0,1:T(8,128)(2,1)S(1)} %get-tuple-element.16), channel_id=1, source_target_pairs={{4,0},{5,1},{6,2},{7,3},{8,4},{9,5},{10,6},{11,7},{12,8},{13,9},{1... | collective-permute-start | bytes 1572872 | tf_op jit(solution)/shard_map/ppermute | solution.py:12
  67.5 9.5 %collective-permute-done.6 = bf16[1024,256]{0,1:T(8,128)(2,1)S(1)} collective-permute-done((bf16[1024,256]{0,1:T(8,128)(2,1)S(1)}, bf16[1024,256]{0,1:T(8,128)(2,1)S(1)}, u32[]{:S(2)}, u32[]{:S(2)}) %collective-permute-start.6) | collective-permute-done | bytes 524320 | tf_op jit(solution)/shard_map/ppermute | solution.py:12
  77.0 12.0 %collective-permute-done.7 = bf16[1024,256]{0,1:T(8,128)(2,1)S(1)} collective-permute-done((bf16[1024,256]{0,1:T(8,128)(2,1)S(1)}, bf16[1024,256]{0,1:T(8,128)(2,1)S(1)}, u32[]{:S(2)}, u32[]{:S(2)}) %collective-permute-start.7) | collective-permute-done | bytes 524320 | tf_op jit(solution)/shard_map/ppermute | solution.py:12
  90.8 8.3 %collective-permute-start.8 = (bf16[1024,256]{0,1:T(8,128)(2,1)S(1)}, bf16[1024,256]{0,1:T(8,128)(2,1)S(1)}, u32[]{:S(2)}, u32[]{:S(2)}) collective-permute-start(bf16[1024,256]{0,1:T(8,128)(2,1)S(1)} %get-tuple-element.18), channel_id=1, source_target_pairs={{0,8},{1,9},{2,10},{3,11},{4,12},{5,13},{6,14},{7,15},{8,16},{9,17... | collective-permute-start | bytes 1572872 | tf_op jit(solution)/shard_map/ppermute | solution.py:12
  99.1 2.3 %collective-permute-start.9 = (bf16[1024,256]{0,1:T(8,128)(2,1)S(1)}, bf16[1024,256]{0,1:T(8,128)(2,1)S(1)}, u32[]{:S(2)}, u32[]{:S(2)}) collective-permute-start(bf16[1024,256]{0,1:T(8,128)(2,1)S(1)} %get-tuple-element.18), channel_id=1, source_target_pairs={{8,0},{9,1},{10,2},{11,3},{12,4},{13,5},{14,6},{15,7},{16,8},{17,9... | collective-permute-start | bytes 1572872 | tf_op jit(solution)/shard_map/ppermute | solution.py:12
  102.1 32.2 %collective-permute-done.8 = bf16[1024,256]{0,1:T(8,128)(2,1)S(1)} collective-permute-done((bf16[1024,256]{0,1:T(8,128)(2,1)S(1)}, bf16[1024,256]{0,1:T(8,128)(2,1)S(1)}, u32[]{:S(2)}, u32[]{:S(2)}) %collective-permute-start.8) | collective-permute-done | bytes 524320 | tf_op jit(solution)/shard_map/ppermute | solution.py:12
  134.3 16.5 %collective-permute-done.9 = bf16[1024,256]{0,1:T(8,128)(2,1)S(1)} collective-permute-done((bf16[1024,256]{0,1:T(8,128)(2,1)S(1)}, bf16[1024,256]{0,1:T(8,128)(2,1)S(1)}, u32[]{:S(2)}, u32[]{:S(2)}) %collective-permute-start.9) | collective-permute-done | bytes 524320 | tf_op jit(solution)/shard_map/ppermute | solution.py:12
  150.8 1.0 convolution_add_fusion.1
  152.6 1.9 %collective-permute-start.10 = (bf16[1024,256]{0,1:T(8,128)(2,1)S(1)}, bf16[1024,256]{0,1:T(8,128)(2,1)S(1)}, u32[]{:S(2)}, u32[]{:S(2)}) collective-permute-start(bf16[1024,256]{0,1:T(8,128)(2,1)S(1)} %get-tuple-element.20), channel_id=1, source_target_pairs={{0,16},{1,17},{2,18},{3,19},{4,20},{5,21},{6,22},{7,23},{8,24},{9,... | collective-permute-start | bytes 1572872 | tf_op jit(solution)/shard_map/ppermute | solution.py:12
  154.5 3.9 %collective-permute-start.11 = (bf16[1024,256]{0,1:T(8,128)(2,1)S(1)}, bf16[1024,256]{0,1:T(8,128)(2,1)S(1)}, u32[]{:S(2)}, u32[]{:S(2)}) collective-permute-start(bf16[1024,256]{0,1:T(8,128)(2,1)S(1)} %get-tuple-element.20), channel_id=1, source_target_pairs={{16,0},{17,1},{18,2},{19,3},{20,4},{21,5},{22,6},{23,7},{24,8},{25... | collective-permute-start | bytes 1572872 | tf_op jit(solution)/shard_map/ppermute | solution.py:12
  159.1 8.2 %collective-permute-done.10 = bf16[1024,256]{0,1:T(8,128)(2,1)S(1)} collective-permute-done((bf16[1024,256]{0,1:T(8,128)(2,1)S(1)}, bf16[1024,256]{0,1:T(8,128)(2,1)S(1)}, u32[]{:S(2)}, u32[]{:S(2)}) %collective-permute-start.10) | collective-permute-done | bytes 524320 | tf_op jit(solution)/shard_map/ppermute | solution.py:12
  167.3 4.0 %collective-permute-done.11 = bf16[1024,256]{0,1:T(8,128)(2,1)S(1)} collective-permute-done((bf16[1024,256]{0,1:T(8,128)(2,1)S(1)}, bf16[1024,256]{0,1:T(8,128)(2,1)S(1)}, u32[]{:S(2)}, u32[]{:S(2)}) %collective-permute-start.11) | collective-permute-done | bytes 524320 | tf_op jit(solution)/shard_map/ppermute | solution.py:12
  171.3 1.0 convolution_add_fusion
  172.8 1.3 convolution_add_fusion.6
  174.4 1.3 copy.9
  (34 shorter events, 8.2 us)
Async XLA Ops:
  0.6 10.8 %copy-start = (f32[1024,256]{1,0:T(8,128)S(1)}, f32[1024,256]{1,0:T(8,128)}, u32[]{:S(2)}) copy-start(f32[1024,256]{1,0:T(8,128)} %param.5) | copy-start | bytes 3145732
  0.6 11.2 %copy-start.3 = (f32[6,512]{1,0:T(8,128)S(1)}, f32[6,512]{1,0:T(8,128)}, u32[]{:S(2)}) copy-start(f32[6,512]{1,0:T(8,128)} %param.7) | copy-start | bytes 36868
  2.1 11.5 %collective-permute-start = (bf16[512,256]{1,0:T(8,128)(2,1)S(1)}, bf16[512,256]{1,0:T(8,128)(2,1)S(1)}, u32[]{:S(2)}, u32[]{:S(2)}) collective-permute-start(bf16[512,256]{1,0:T(8,128)(2,1)S(1)} %get-tuple-element.4), channel_id=1, source_target_pairs={{0,1},{1,2},{2,3},{3,4},{4,5},{5,6},{6,7},{7,8},{8,9},{9,10},{10,1... | collective-permute-start | bytes 786440 | tf_op jit(solution)/shard_map/ppermute | solution.py:12
  4.0 11.3 %collective-permute-start.1 = (bf16[512,256]{1,0:T(8,128)(2,1)S(1)}, bf16[512,256]{1,0:T(8,128)(2,1)}, u32[]{:S(2)}, u32[]{:S(2)}) collective-permute-start(bf16[512,256]{1,0:T(8,128)(2,1)S(1)} %get-tuple-element.5), channel_id=1, source_target_pairs={{1,0},{2,1},{3,2},{4,3},{5,4},{6,5},{7,6},{8,7},{9,8},{10,9},{11,1... | collective-permute-start | bytes 786440 | tf_op jit(solution)/shard_map/ppermute | solution.py:12
  17.5 1.1 copy-start.1
  18.7 37.8 %slice-start = ((s8[4718592]{0:T(1024)(128)(4,1)}), s8[4194304]{0:T(1024)(128)(4,1)S(1)}, s32[]{:S(2)}) async-start(s8[4718592]{0:T(1024)(128)(4,1)} %bitcast.88), calls=%async_computation | async-start | bytes 8388608
  19.0 13.2 %collective-permute-start.2 = (bf16[1024,256]{0,1:T(8,128)(2,1)S(1)}, bf16[1024,256]{0,1:T(8,128)(2,1)S(1)}, u32[]{:S(2)}, u32[]{:S(2)}) collective-permute-start(bf16[1024,256]{0,1:T(8,128)(2,1)S(1)} %get-tuple-element.12), channel_id=1, source_target_pairs={{0,1},{1,2},{2,3},{3,4},{4,5},{5,6},{6,7},{7,8},{8,9},{9,10},{10,1... | collective-permute-start | bytes 1572872 | tf_op jit(solution)/shard_map/ppermute | solution.py:12
  21.2 12.7 %collective-permute-start.3 = (bf16[1024,256]{0,1:T(8,128)(2,1)S(1)}, bf16[1024,256]{0,1:T(8,128)(2,1)S(1)}, u32[]{:S(2)}, u32[]{:S(2)}) collective-permute-start(bf16[1024,256]{0,1:T(8,128)(2,1)S(1)} %get-tuple-element.12), channel_id=1, source_target_pairs={{1,0},{2,1},{3,2},{4,3},{5,4},{6,5},{7,6},{8,7},{9,8},{10,9},{11,1... | collective-permute-start | bytes 1572872 | tf_op jit(solution)/shard_map/ppermute | solution.py:12
  33.9 22.6 %slice-start.1 = ((s8[4718592]{0:T(1024)(128)(4,1)}), s8[524288]{0:T(1024)(128)(4,1)S(1)}, s32[]{:S(2)}) async-start(s8[4718592]{0:T(1024)(128)(4,1)} %bitcast.88), calls=%async_computation.1 | async-start | bytes 1048576
  36.9 18.4 %collective-permute-start.4 = (bf16[1024,256]{0,1:T(8,128)(2,1)S(1)}, bf16[1024,256]{0,1:T(8,128)(2,1)S(1)}, u32[]{:S(2)}, u32[]{:S(2)}) collective-permute-start(bf16[1024,256]{0,1:T(8,128)(2,1)S(1)} %get-tuple-element.14), channel_id=1, source_target_pairs={{0,2},{1,3},{2,4},{3,5},{4,6},{5,7},{6,8},{7,9},{8,10},{9,11},{10,... | collective-permute-start | bytes 1572872 | tf_op jit(solution)/shard_map/ppermute | solution.py:12
  38.9 17.6 %collective-permute-start.5 = (bf16[1024,256]{0,1:T(8,128)(2,1)S(1)}, bf16[1024,256]{0,1:T(8,128)(2,1)S(1)}, u32[]{:S(2)}, u32[]{:S(2)}) collective-permute-start(bf16[1024,256]{0,1:T(8,128)(2,1)S(1)} %get-tuple-element.14), channel_id=1, source_target_pairs={{2,0},{3,1},{4,2},{5,3},{6,4},{7,5},{8,6},{9,7},{10,8},{11,9},{12,... | collective-permute-start | bytes 1572872 | tf_op jit(solution)/shard_map/ppermute | solution.py:12
  58.0 9.2 %copy-start.2 = (bf16[6,256,256]{2,1,0:T(8,128)(2,1)S(1)}, bf16[6,256,256]{2,1,0:T(8,128)(2,1)}, u32[]{:S(2)}) copy-start(bf16[6,256,256]{2,1,0:T(8,128)(2,1)} %param.9) | copy-start | bytes 2359300
  58.3 18.7 %collective-permute-start.6 = (bf16[1024,256]{0,1:T(8,128)(2,1)S(1)}, bf16[1024,256]{0,1:T(8,128)(2,1)S(1)}, u32[]{:S(2)}, u32[]{:S(2)}) collective-permute-start(bf16[1024,256]{0,1:T(8,128)(2,1)S(1)} %get-tuple-element.16), channel_id=1, source_target_pairs={{0,4},{1,5},{2,6},{3,7},{4,8},{5,9},{6,10},{7,11},{8,12},{9,13},{1... | collective-permute-start | bytes 1572872 | tf_op jit(solution)/shard_map/ppermute | solution.py:12
  61.0 28.0 %collective-permute-start.7 = (bf16[1024,256]{0,1:T(8,128)(2,1)S(1)}, bf16[1024,256]{0,1:T(8,128)(2,1)S(1)}, u32[]{:S(2)}, u32[]{:S(2)}) collective-permute-start(bf16[1024,256]{0,1:T(8,128)(2,1)S(1)} %get-tuple-element.16), channel_id=1, source_target_pairs={{4,0},{5,1},{6,2},{7,3},{8,4},{9,5},{10,6},{11,7},{12,8},{13,9},{1... | collective-permute-start | bytes 1572872 | tf_op jit(solution)/shard_map/ppermute | solution.py:12
  90.8 43.5 %collective-permute-start.8 = (bf16[1024,256]{0,1:T(8,128)(2,1)S(1)}, bf16[1024,256]{0,1:T(8,128)(2,1)S(1)}, u32[]{:S(2)}, u32[]{:S(2)}) collective-permute-start(bf16[1024,256]{0,1:T(8,128)(2,1)S(1)} %get-tuple-element.18), channel_id=1, source_target_pairs={{0,8},{1,9},{2,10},{3,11},{4,12},{5,13},{6,14},{7,15},{8,16},{9,17... | collective-permute-start | bytes 1572872 | tf_op jit(solution)/shard_map/ppermute | solution.py:12
  99.1 51.7 %collective-permute-start.9 = (bf16[1024,256]{0,1:T(8,128)(2,1)S(1)}, bf16[1024,256]{0,1:T(8,128)(2,1)S(1)}, u32[]{:S(2)}, u32[]{:S(2)}) collective-permute-start(bf16[1024,256]{0,1:T(8,128)(2,1)S(1)} %get-tuple-element.18), channel_id=1, source_target_pairs={{8,0},{9,1},{10,2},{11,3},{12,4},{13,5},{14,6},{15,7},{16,8},{17,9... | collective-permute-start | bytes 1572872 | tf_op jit(solution)/shard_map/ppermute | solution.py:12
  152.6 14.7 %collective-permute-start.10 = (bf16[1024,256]{0,1:T(8,128)(2,1)S(1)}, bf16[1024,256]{0,1:T(8,128)(2,1)S(1)}, u32[]{:S(2)}, u32[]{:S(2)}) collective-permute-start(bf16[1024,256]{0,1:T(8,128)(2,1)S(1)} %get-tuple-element.20), channel_id=1, source_target_pairs={{0,16},{1,17},{2,18},{3,19},{4,20},{5,21},{6,22},{7,23},{8,24},{9,... | collective-permute-start | bytes 1572872 | tf_op jit(solution)/shard_map/ppermute | solution.py:12
  154.5 16.8 %collective-permute-start.11 = (bf16[1024,256]{0,1:T(8,128)(2,1)S(1)}, bf16[1024,256]{0,1:T(8,128)(2,1)S(1)}, u32[]{:S(2)}, u32[]{:S(2)}) collective-permute-start(bf16[1024,256]{0,1:T(8,128)(2,1)S(1)} %get-tuple-element.20), channel_id=1, source_target_pairs={{16,0},{17,1},{18,2},{19,3},{20,4},{21,5},{22,6},{23,7},{24,8},{25... | collective-permute-start | bytes 1572872 | tf_op jit(solution)/shard_map/ppermute | solution.py:12
where the time goes:
time: 176 us
  waiting for transfers between devices  104 us (59%)
  starting transfers between devices  50.9 us (29%)
  matrix products  13.3 us (8%)
  other arithmetic  3.86 us (2%)
  local copies, waits for them, and re-layouts  2.41 us (1%)
    ppermute x12, waiting for transfers between devices, passed_along(): lax.ppermute(value, axis, [(source, source + steps) for source in range(l...  104 us
    ppermute x12, starting transfers between devices, passed_along(): lax.ppermute(value, axis, [(source, source + steps) for source in range(l...  50.9 us
    dot_general x6, matrix products, body(): pre_gate = jnp.dot(joined_rows, weights, preferred_element_type=jnp.float32)  8.44 us
  transfers between devices with their start and end apart: 12, of which 12 were waited for; matrix products, arithmetic and copies ran while one was open for 1% of the time, Pallas kernels for 0%

commit v1 on v0

v1 whole, which is shorter than its diff:
```python
import jax
import jax.numpy as jnp
from jax import lax
from jax.sharding import PartitionSpec as P

LAYERS = 6
FIRST_DILATION = 512


def shifted(value, rows):
    padding = jnp.zeros((abs(rows),) + value.shape[1:], value.dtype)
    if rows > 0:
        return jnp.concatenate([padding, value[:-rows]], 0)
    return jnp.concatenate([value[-rows:], padding], 0)


def body(devices, signal, conv_weight, conv_bias, res_weight, skip_weight):
    row_count, channels = signal.shape
    halves = row_count // FIRST_DILATION
    own = FIRST_DILATION // devices
    sent = signal.astype(jnp.bfloat16).reshape(halves, devices, own, channels).transpose(1, 0, 2, 3)
    taken = lax.all_to_all(sent.reshape(devices, halves * own, channels), "seq", 0, 0, tiled=True)
    start = taken.reshape(row_count, channels).astype(jnp.float32)
    delta = jnp.zeros_like(start)
    skip_sum = jnp.zeros_like(start)
    for layer in range(LAYERS):
        rounded = (start + delta).astype(jnp.bfloat16)
        step = own * 2**layer
        joined = jnp.concatenate([shifted(rounded, step), rounded, shifted(rounded, -step)], 1)
        pre_gate = jnp.dot(joined, conv_weight[layer], preferred_element_type=jnp.float32) + conv_bias[layer]
        gated = (jnp.tanh(pre_gate[:, :channels]) * jax.nn.sigmoid(pre_gate[:, channels:])).astype(jnp.bfloat16)
        delta = delta + jnp.dot(gated, res_weight[layer], preferred_element_type=jnp.float32)
        skip_sum = skip_sum + jnp.dot(gated, skip_weight[layer], preferred_element_type=jnp.float32)
    both = jnp.concatenate([delta, skip_sum], 1).astype(jnp.bfloat16)
    back = lax.all_to_all(both.reshape(devices, halves * own, 2 * channels), "seq", 0, 0, tiled=True)
    back = back.reshape(devices, halves, own, 2 * channels).transpose(1, 0, 2, 3).reshape(row_count, 2 * channels)
    back = back.astype(jnp.float32)
    return signal + back[:, :channels], back[:, channels:]


def solution(mesh):
    devices = mesh.shape["seq"]
    in_specs = (P("seq", None), P(), P(), P(), P())
    out_specs = (P("seq", None), P("seq", None))

    def run(*args):
        return body(devices, *args)

    return jax.shard_map(run, mesh=mesh, in_specs=in_specs, out_specs=out_specs, check_vma=False)
```

time: 176 us -> 105 us (0.60)
  the two profiles are of different devices: /device:TPU:22 before, /device:TPU:1 now
where the time goes in v1:
time: 105 us
  blocking collectives  38.4 us (37%)
  waiting for transfers between devices  21.4 us (20%)
  starting transfers between devices  15.7 us (15%)
  matrix products  10.7 us (10%)
  local copies, waits for them, and re-layouts  10.6 us (10%)
  other arithmetic  7.12 us (7%)
    all_to_all x1, blocking collectives, body(): lax.all_to_all(both.reshape(devices, halves * own, 2 * channels), 'seq',...  38.4 us
    all_to_all x1, waiting for transfers between devices, body(): lax.all_to_all(sent.reshape(devices, halves * own, channels), 'seq', 0, 0...  21.4 us
    all_to_all x1, starting transfers between devices, body(): lax.all_to_all(sent.reshape(devices, halves * own, channels), 'seq', 0, 0...  15.7 us
    convert_element_type x3, local copies, waits for them, and re-layouts, body(): back = back.astype(jnp.float32)  7.29 us
    dot_general x6, matrix products, body(): jnp.dot(joined, conv_weight[layer], preferred_element_type=jnp.float32)  7.14 us
    slice x1, other arithmetic, body(): return (signal + back[:, :channels], back[:, channels:])  2.74 us
    convert_element_type x6, other arithmetic, body(): (jnp.tanh(pre_gate[:, :channels]) * jax.nn.sigmoid(pre_gate[:, channels:]...  2.65 us
  transfers between devices with their start and end apart: 1, of which 1 were waited for; matrix products, arithmetic and copies ran while one was open for 0% of the time, Pallas kernels for 0%

profile of v1, /device:TPU:1, one launch (start us, length us, event | category | flops | bytes accessed | tf_op | source)
XLA Modules:
  0.0 104.8 jit_solution(12823507597824222265)
XLA Ops:
  0.6 1.3 %convert_element_type.54 = bf16[1024,256]{1,0:T(8,128)(2,1)S(1)} convert(f32[1024,256]{1,0:T(8,128)} %param.5) | non-fusion elementwise | flops 262144 | bytes 1572864 | tf_op jit(solution)/shard_map/convert_element_type | solution.py:21
  2.1 0.4 copy.7
  2.5 1.1 %reshape.25 = bf16[256,4,256]{2,1,0:T(4,128)(2,1)} reshape(bf16[256,2,2,256]{3,2,1,0:T(2,128)(2,1)S(1)} %copy.7) | data formatting | bytes 1048576 | tf_op jit(solution)/shard_map/reshape | solution.py:22
  3.6 15.7 %all-to-all-start = ((bf16[256,4,256]{2,1,0:T(4,128)(2,1)}), bf16[256,4,256]{2,1,0:T(4,128)(2,1)S(1)}, u32[]{:S(2)}, u32[]{:S(2)}) async-start(bf16[256,4,256]{2,1,0:T(4,128)(2,1)} %reshape.25), calls=%async_computation | async-start | bytes 1048576 | tf_op jit(solution)/shard_map/all_to_all | solution.py:22
  19.3 21.4 %all-to-all-done = bf16[256,4,256]{2,1,0:T(4,128)(2,1)S(1)} async-done(((bf16[256,4,256]{2,1,0:T(4,128)(2,1)}), bf16[256,4,256]{2,1,0:T(4,128)(2,1)S(1)}, u32[]{:S(2)}, u32[]{:S(2)}) %all-to-all-start) | async-done | bytes 524320 | tf_op jit(solution)/shard_map/all_to_all | solution.py:22
  41.0 2.3 %convolution_add_fusion.5 = f32[1024,512]{1,0:T(8,128)S(1)} fusion(bf16[1022,256]{1,0:T(8,128)(2,1)S(1)} %get-tuple-element.15, bf16[1022,256]{1,0:T(8,128)(2,1)S(1)} %get-tuple-element.14, bf16[1024,256]{1,0:T(8,128)(2,1)S(1)} %reshape.26, f32[512]{0:T(512)S(1)} %bitcast.93, bf16[6,768,512]{2,1,0:T(8,128)(2,1)} %param.6), kind=kOutput, calls=%fused_computation.25 | convolution fusion | flops 813694976 | bytes 4456448 | tf_op jit(solution)/shard_map/dot_general | solution.py:30
  43.2 0.4 fusion.97
  43.7 0.7 copy-done
  44.7 0.3 fusion.68
  45.2 1.0 convolution_add_fusion.4
  46.2 0.4 fusion.98
  46.9 0.3 fusion.69
  47.3 1.0 convolution_add_fusion.3
  48.3 0.4 fusion.99
  49.0 0.3 fusion.70
  49.4 1.0 convolution_add_fusion.2
  50.4 0.4 fusion.100
  51.1 0.3 fusion.71
  51.5 1.0 convolution_add_fusion.1
  52.5 0.4 fusion.101
  52.9 0.3 convolution_add_fusion.7
  53.2 0.3 fusion.72
  53.6 1.0 convolution_add_fusion
  54.6 0.4 fusion.102
  55.0 0.3 fusion.67
  55.3 0.3 fusion.66
  55.9 0.5 pad_maximum_fusion
  56.4 38.4 %all_to_all.10 = bf16[256,4,512]{2,1,0:T(4,128)(2,1)} all-to-all(bf16[256,4,512]{2,1,0:T(4,128)(2,1)S(1)} %pad_maximum_fusion), channel_id=1, replica_groups=mesh['seq'=256] {'seq'}, dimensions={0} | all-to-all | bytes 2097152 | tf_op jit(solution)/shard_map/all_to_all | solution.py:35
  94.8 2.5 %reshape.28 = f32[256,2,2,512]{3,2,1,0:T(2,128)S(1)} reshape(bf16[256,4,512]{2,1,0:T(4,128)(2,1)} %all_to_all.10) | data formatting | bytes 3145728 | tf_op jit(solution)/shard_map/convert_element_type | solution.py:37
  97.3 2.1 %copy.10 = f32[256,2,2,512]{3,2,0,1:T(2,128)} copy(f32[256,2,2,512]{3,2,1,0:T(2,128)S(1)} %reshape.28) | data formatting | bytes 4194304 | tf_op jit(solution)/shard_map/convert_element_type | solution.py:37
  99.4 2.7 %reshape.27 = f32[1024,512]{1,0:T(8,128)S(1)} reshape(f32[2,256,2,512]{3,2,1,0:T(2,128)} %bitcast.86) | data formatting | bytes 4194304 | tf_op jit(solution)/shard_map/convert_element_type | solution.py:37
  102.1 2.7 %fusion.171 = (f32[1024,256]{1,0:T(8,128)}, f32[1024,256]{1,0:T(8,128)}) fusion(f32[1024,512]{1,0:T(8,128)S(1)} %reshape.27, f32[1024,256]{1,0:T(8,128)} %param.5), kind=kLoop, calls=%fused_computation.197 | loop fusion | flops 262144 | bytes 5242880 | tf_op jit(solution)/shard_map/slice | solution.py:38
  (25 shorter events, 2.4 us)
Async XLA Ops:
  1.9 17.3 %copy-start.2 = (f32[6,512]{1,0:T(8,128)S(1)}, f32[6,512]{1,0:T(8,128)}, u32[]{:S(2)}) copy-start(f32[6,512]{1,0:T(8,128)} %param.7) | copy-start | bytes 36868
  3.6 37.1 %all-to-all-start = ((bf16[256,4,256]{2,1,0:T(4,128)(2,1)}), bf16[256,4,256]{2,1,0:T(4,128)(2,1)S(1)}, u32[]{:S(2)}, u32[]{:S(2)}) async-start(bf16[256,4,256]{2,1,0:T(4,128)(2,1)} %reshape.25), calls=%async_computation | async-start | bytes 1048576 | tf_op jit(solution)/shard_map/all_to_all | solution.py:22
  40.8 4.4 %slice-start = ((s8[4718592]{0:T(1024)(128)(4,1)}), s8[4194304]{0:T(1024)(128)(4,1)S(1)}, s32[]{:S(2)}) async-start(s8[4718592]{0:T(1024)(128)(4,1)} %bitcast.94), calls=%async_computation.2 | async-start | bytes 8388608
  40.9 4.2 %slice-start.1 = ((s8[4718592]{0:T(1024)(128)(4,1)}), s8[524288]{0:T(1024)(128)(4,1)S(1)}, s32[]{:S(2)}) async-start(s8[4718592]{0:T(1024)(128)(4,1)} %bitcast.94), calls=%async_computation.3 | async-start | bytes 1048576
  43.2 1.1 %copy-start = (bf16[6,256,256]{2,1,0:T(8,128)(2,1)S(1)}, bf16[6,256,256]{2,1,0:T(8,128)(2,1)}, u32[]{:S(2)}) copy-start(bf16[6,256,256]{2,1,0:T(8,128)(2,1)} %param.9) | copy-start | bytes 2359300
  43.2 1.4 %copy-start.1 = (bf16[6,256,256]{2,1,0:T(8,128)(2,1)S(1)}, bf16[6,256,256]{2,1,0:T(8,128)(2,1)}, u32[]{:S(2)}) copy-start(bf16[6,256,256]{2,1,0:T(8,128)(2,1)} %param.8) | copy-start | bytes 2359300

commit v2 on v1

v2 whole, which is shorter than its diff:
```python
import jax
import jax.numpy as jnp
from jax import lax
from jax.experimental import pallas as pl
from jax.experimental.pallas import tpu as pltpu
from jax.sharding import PartitionSpec as P

LAYERS = 6
HALVES = 2
RESIDUES = 512
GROUP = 16
CHUNKS = 2
LENGTH = 512
C = 256
PAD = 32
TILE = 256
MESH = pl.DeviceIdType.MESH
BF16 = jnp.bfloat16
F32 = jnp.float32

ALONG_Z = [(dz, dc) for dz in (1, 7, 2, 6, 3, 5, 4, 0) for dc in (0, 1) if (dz, dc) != (0, 0)]
ACROSS = [(dy, dx) for dy in (0, 1, 3, 2) for dx in (1, 3, 2, 0) if (dy, dx) != (0, 0)]


def kernel(
    signal_hbm,
    conv_hbm,
    bias_ref,
    res_hbm,
    skip_hbm,
    delta_out,
    skip_out,
    signal,
    conv,
    proj,
    sent,
    perm,
    perm_t,
    r1,
    t1,
    r2,
    t2,
    r3,
    t3,
    cur,
    skip,
    x3,
    load_sem,
    weight_sem,
    send_sem,
    in_z_sem,
    in_xy_sem,
    out_xy_sem,
    out_z_sem,
    own_sem,
):
    me = lax.axis_index("seq")
    j, g = lax.rem(me, GROUP), me // GROUP
    z, core = j // 2, lax.rem(j, 2)
    y, x = g // 4, lax.rem(g, 4)
    z_peers = [lax.rem(z + dz, 8) * 2 + lax.rem(core + dc, 2) for dz, dc in ALONG_Z]
    xy_peers = [lax.rem(y + dy, 4) * 4 + lax.rem(x + dx, 4) for dy, dx in ACROSS]

    barrier = pltpu.get_barrier_semaphore()
    for peer in z_peers:
        pl.semaphore_signal(barrier, inc=1, device_id=(g * GROUP + peer,), device_id_type=MESH)
    for peer in xy_peers:
        pl.semaphore_signal(barrier, inc=1, device_id=(peer * GROUP + j,), device_id_type=MESH)

    load = pltpu.make_async_copy(signal_hbm, signal, load_sem)
    load.start()
    weights = [
        pltpu.make_async_copy(conv_hbm, conv, weight_sem.at[0]),
        pltpu.make_async_copy(res_hbm, proj.at[:, :, pl.ds(0, C)], weight_sem.at[1]),
        pltpu.make_async_copy(skip_hbm, proj.at[:, :, pl.ds(C, C)], weight_sem.at[2]),
    ]
    for copy in weights:
        copy.start()
    row = lax.broadcasted_iota(jnp.int32, (LENGTH, LENGTH), 0)
    col = lax.broadcasted_iota(jnp.int32, (LENGTH, LENGTH), 1)
    perm[...] = jnp.where(col == (row & 31) * 16 + (row >> 5), 1.0, 0.0).astype(BF16)
    perm_t[...] = jnp.where(row == (col & 31) * 16 + (col >> 5), 1.0, 0.0).astype(BF16)
    cur[pl.ds(0, PAD), :] = jnp.zeros((PAD, C), F32)
    cur[pl.ds(PAD + LENGTH, PAD), :] = jnp.zeros((PAD, C), F32)
    load.wait()
    sent[...] = signal[...].astype(BF16)
    pl.semaphore_wait(barrier, 2 * (GROUP - 1))

    def rows_of(s, peer):
        return pl.ds(pl.multiple_of(s * 256 + peer * 16, 16), 16)

    def send(src, dst, stage, recv, device):
        pltpu.make_async_remote_copy(
            src_ref=src,
            dst_ref=dst,
            send_sem=send_sem.at[stage],
            recv_sem=recv,
            device_id=(device,),
            device_id_type=MESH,
        ).start()

    def arrived(buffer, sem):
        part = buffer.at[pl.ds(0, GROUP - 1)]
        pltpu.make_async_copy(part, part, sem).wait()

    for s in range(CHUNKS):
        for peer in z_peers:
            send(sent.at[:, rows_of(s, peer), :], r1.at[s, j], s, in_z_sem.at[s], g * GROUP + peer)
        r1[s, j] = sent[:, rows_of(s, j), :]

    def spread(s):
        arrived(r1.at[s], in_z_sem.at[s])
        rows = jnp.dot(perm[...], r1[s].reshape(LENGTH, C), preferred_element_type=F32)
        t1[s] = rows.astype(BF16).reshape(GROUP, 32, C)
        for peer in xy_peers:
            send(t1.at[s, peer], r2.at[s, g], 2 + s, in_xy_sem.at[s], peer * GROUP + j)
        r2[s, g] = t1[s, g]

    def layers(s):
        arrived(r2.at[s], in_xy_sem.at[s])
        cur[pl.ds(PAD, LENGTH), :] = r2[s].reshape(LENGTH, C).astype(F32)
        for layer in range(LAYERS):
            d = 2**layer
            for tap in range(3):
                x3[:, pl.ds(tap * C, C)] = cur[pl.ds(PAD + (tap - 1) * d, LENGTH), :].astype(BF16)
            for tile in range(LENGTH // TILE):
                at = pl.ds(tile * TILE, TILE)
                pre = jnp.dot(x3[at, :], conv[layer], preferred_element_type=F32)
                pre = pre + bias_ref[pl.ds(layer, 1), :]
                gated = (jnp.tanh(pre[:, :C]) * (0.5 + 0.5 * jnp.tanh(0.5 * pre[:, C:]))).astype(BF16)
                both = jnp.dot(gated, proj[layer], preferred_element_type=F32)
                at_cur = pl.ds(PAD + tile * TILE, TILE)
                if layer < LAYERS - 1:
                    cur[at_cur, :] = cur[at_cur, :] + both[:, :C]
                    skip[at, :] = both[:, C:] if layer == 0 else skip[at, :] + both[:, C:]
                else:
                    slots = pl.ds(tile * TILE // 32, TILE // 32)
                    start = r2[s, slots].reshape(TILE, C).astype(F32)
                    delta = (cur[at_cur, :] - start) + both[:, :C]
                    t2[s, 0, slots] = delta.astype(BF16).reshape(TILE // 32, 32, C)
                    total = skip[at, :] + both[:, C:]
                    t2[s, 1, slots] = total.astype(BF16).reshape(TILE // 32, 32, C)
        for part in range(2):
            for peer in xy_peers:
                send(
                    t2.at[s, part, peer],
                    r3.at[s, part, g],
                    4 + 2 * s + part,
                    out_xy_sem.at[2 * s + part],
                    peer * GROUP + j,
                )
            r3[s, part, g] = t2[s, part, g]

    own = []
    outs = (delta_out, skip_out)

    def give_back(s, part):
        arrived(r3.at[s, part], out_xy_sem.at[2 * s + part])
        rows = jnp.dot(perm_t[...], r3[s, part].reshape(LENGTH, C), preferred_element_type=F32)
        t3[s, part] = rows.astype(BF16).reshape(GROUP, HALVES, 16, C)
        for peer in z_peers:
            send(
                t3.at[s, part, peer],
                outs[part].at[:, rows_of(s, j), :],
                8 + 2 * s + part,
                out_z_sem.at[2 * s + part],
                g * GROUP + peer,
            )
        copy = pltpu.make_async_copy(
            t3.at[s, part, j], outs[part].at[:, rows_of(s, j), :], own_sem.at[2 * s + part]
        )
        copy.start()
        own.append(copy)

    spread(0)
    for copy in weights:
        copy.wait()
    layers(0)
    spread(1)
    give_back(0, 0)
    give_back(0, 1)
    layers(1)
    give_back(1, 0)
    give_back(1, 1)

    for s in range(CHUNKS):
        for part in range(2):
            arrived(t3.at[s, part], out_z_sem.at[2 * s + part])
    for copy in own:
        copy.wait()
    for stage in range(12):
        arrived(t1.at[0], send_sem.at[stage])


def body(signal, conv_weight, conv_bias, res_weight, skip_weight):
    any_space = pl.BlockSpec(memory_space=pl.ANY)
    slab = (CHUNKS, GROUP, 32, C)
    delta, skip_sum = pl.pallas_call(
        kernel,
        out_shape=[jax.ShapeDtypeStruct((HALVES, RESIDUES, C), BF16)] * 2,
        in_specs=[any_space, any_space, pl.BlockSpec(memory_space=pltpu.VMEM), any_space, any_space],
        out_specs=[any_space, any_space],
        scratch_shapes=[
            pltpu.VMEM((HALVES, RESIDUES, C), F32),
            pltpu.VMEM((LAYERS, 3 * C, 2 * C), BF16),
            pltpu.VMEM((LAYERS, C, 2 * C), BF16),
            pltpu.VMEM((HALVES, RESIDUES, C), BF16),
            pltpu.VMEM((LENGTH, LENGTH), BF16),
            pltpu.VMEM((LENGTH, LENGTH), BF16),
            pltpu.VMEM((CHUNKS, GROUP, HALVES, 16, C), BF16),
            pltpu.VMEM(slab, BF16),
            pltpu.VMEM(slab, BF16),
            pltpu.VMEM((CHUNKS, 2, GROUP, 32, C), BF16),
            pltpu.VMEM((CHUNKS, 2, GROUP, 32, C), BF16),
            pltpu.VMEM((CHUNKS, 2, GROUP, HALVES, 16, C), BF16),
            pltpu.VMEM((LENGTH + 2 * PAD, C), F32),
            pltpu.VMEM((LENGTH, C), F32),
            pltpu.VMEM((LENGTH, 3 * C), BF16),
            pltpu.SemaphoreType.DMA,
            pltpu.SemaphoreType.DMA((3,)),
            pltpu.SemaphoreType.DMA((12,)),
            pltpu.SemaphoreType.DMA((2,)),
            pltpu.SemaphoreType.DMA((2,)),
            pltpu.SemaphoreType.DMA((4,)),
            pltpu.SemaphoreType.DMA((4,)),
            pltpu.SemaphoreType.DMA((4,)),
        ],
        compiler_params=pltpu.CompilerParams(
            collective_id=0, has_side_effects=True, vmem_limit_bytes=60 * 2**20
        ),
    )(
        signal.reshape(HALVES, RESIDUES, C),
        conv_weight,
        conv_bias,
        res_weight,
        skip_weight,
    )
    shape = signal.shape
    return signal + delta.reshape(shape).astype(F32), skip_sum.reshape(shape).astype(F32)


def solution(mesh):
    in_specs = (P("seq", None), P(), P(), P(), P())
    out_specs = (P("seq", None), P("seq", None))
    return jax.shard_map(body, mesh=mesh, in_specs=in_specs, out_specs=out_specs, check_vma=False)
```

time: 105 us -> 76.6 us (0.73)
  Pallas kernels: 0 us -> 71.6 us
  blocking collectives: 38.4 us -> 0 us
  waiting for transfers between devices: 21.4 us -> 0 us
  starting transfers between devices: 15.7 us -> 0 us
  matrix products: 10.7 us -> 0 us
  local copies, waits for them, and re-layouts: 10.6 us -> 0.01 us
  other arithmetic: 7.12 us -> 4.2 us
    pallas_call x0 -> x1, Pallas kernels: none -> 71.6 us  [body(): pl.pallas_call(kernel, out_shape=[jax.ShapeDtypeStruct((HALVES, RESIDUES,...]
    all_to_all x1 -> x0, blocking collectives: 38.4 us -> none  [body(): lax.all_to_all(both.reshape(devices, halves * own, 2 * channels), 'seq',...]
    all_to_all x1 -> x0, waiting for transfers between devices: 21.4 us -> none  [body(): lax.all_to_all(sent.reshape(devices, halves * own, channels), 'seq', 0, 0...]
    all_to_all x1 -> x0, starting transfers between devices: 15.7 us -> none  [body(): lax.all_to_all(sent.reshape(devices, halves * own, channels), 'seq', 0, 0...]
    dot_general x18 -> x0, matrix products: 10.7 us -> none  [the longest x6 7.14 us: body(): jnp.dot(joined, conv_weight[layer], preferred_element_type=jnp.float32)]
    convert_element_type x3 -> x0, local copies, waits for them, and re-layouts: 7.29 us -> none  [body(): back = back.astype(jnp.float32)]
    slice x1 -> x0, other arithmetic: 2.74 us -> none  [body(): return (signal + back[:, :channels], back[:, channels:])]
    add x0 -> x1, other arithmetic: none -> 2.11 us  [body(): signal + delta.reshape(shape).astype(F32)]
  transfers between devices with their start and end apart: 1 -> 0, of which waited for: 1 -> 0; matrix products, arithmetic and copies ran while one was open for 0% -> 0% of each run, Pallas kernels for 0% -> 0%
where the time goes in v2:
time: 76.6 us; the launch traced here: 76.4 us
  Pallas kernels  71.6 us (93%)
  other arithmetic  4.2 us (5%)
    pallas_call x1, Pallas kernels, body(): pl.pallas_call(kernel, out_shape=[jax.ShapeDtypeStruct((HALVES, RESIDUES,...  71.6 us
    add x1, other arithmetic, body(): signal + delta.reshape(shape).astype(F32)  2.11 us
    convert_element_type x1, other arithmetic, body(): skip_sum.reshape(shape).astype(F32)  2.09 us

profile of v2, /device:TPU:1, one launch (start us, length us, event | category | flops | bytes accessed | tf_op | source)
XLA Modules:
  0.0 76.4 jit_solution(7510544312858631522)
XLA Ops:
  0.6 0.0 copy-start
  0.6 71.6 %shard_map.68 = (bf16[2,512,256]{2,1,0:T(8,128)(2,1)}, bf16[2,512,256]{2,1,0:T(8,128)(2,1)}) custom-call(f32[2,512,256]{2,1,0:T(8,128)} %bitcast.7, bf16[6,768,512]{2,1,0:T(8,128)(2,1)} %conv_hbm.1, f32[6,512]{1,0:T(8,128)} %bias_ref.1, bf16[6,256,256]{2,1,0:T(8,128)(2,1)} %res_hbm.1, bf16[6,256,256]{2,1,0:T(8,128)(2,1)} %skip_hbm.1), custom_call_target="tpu_custom_call" | custom-call | tf_op jit(solution)/shard_map/pallas_call | solution.py:198
  72.2 0.0 copy-done
  72.2 2.1 %convert_add_fusion = f32[1024,256]{1,0:T(8,128)} fusion(f32[1024,256]{1,0:T(8,128)S(1)} %copy-done, bf16[2,512,256]{2,1,0:T(8,128)(2,1)} %get-tuple-element.4), kind=kLoop, calls=%fused_computation | loop fusion | flops 524288 | bytes 2621440 | tf_op jit(solution)/shard_map/add | solution.py:239
  74.4 2.1 %bitcast_convert_fusion = f32[1024,256]{1,0:T(8,128)} fusion(bf16[2,512,256]{2,1,0:T(8,128)(2,1)} %get-tuple-element.5), kind=kLoop, calls=%fused_computation.1 | loop fusion | flops 262144 | bytes 1572864 | tf_op jit(solution)/shard_map/convert_element_type | solution.py:239
Async XLA Ops:
  0.6 71.6 %copy-start = (f32[1024,256]{1,0:T(8,128)S(1)}, f32[1024,256]{1,0:T(8,128)}, u32[]{:S(2)}) copy-start(f32[1024,256]{1,0:T(8,128)} %param.5) | copy-start | bytes 3145732

commit v3 on v2

v3 whole, which is shorter than its diff:
```python
import jax
import jax.numpy as jnp
from jax import lax
from jax.experimental import pallas as pl
from jax.experimental.pallas import tpu as pltpu
from jax.sharding import PartitionSpec as P

LAYERS = 6
HALVES = 2
RESIDUES = 512
GROUP = 16
LENGTH = 512
C = 256
PAD = 32
TILE = 256
MESH = pl.DeviceIdType.MESH
BF16 = jnp.bfloat16
F32 = jnp.float32

ALONG_Z = [(dz, dc) for dz in (1, 7, 2, 6, 3, 5, 4, 0) for dc in (0, 1) if (dz, dc) != (0, 0)]
ACROSS = [(dy, dx) for dy in (0, 1, 3, 2) for dx in (1, 3, 2, 0) if (dy, dx) != (0, 0)]


def one_hot(rows, source):
    out = lax.broadcasted_iota(jnp.int32, (rows, rows), 0)
    col = lax.broadcasted_iota(jnp.int32, (rows, rows), 1)
    return jnp.where(col == source(out), 1.0, 0.0).astype(BF16)


def reordered(matrix, rows):
    return jnp.dot(matrix, rows, preferred_element_type=F32)


def kernel(
    signal_hbm,
    conv_hbm,
    bias_ref,
    res_hbm,
    skip_hbm,
    delta_out,
    skip_out,
    signal,
    conv,
    proj,
    swap256,
    split512,
    join512,
    turn512,
    enter512,
    sent_xy,
    sent_z,
    sent_late,
    first_xy,
    first_z,
    next_z,
    next_xy,
    halves,
    late_z,
    late_next,
    late,
    leave,
    passing,
    last,
    cur,
    skip,
    start,
    result,
    x3,
    load_sem,
    weight_sem,
    send_sem,
    recv_sem,
    own_sem,
):
    me = lax.axis_index("seq")
    j, g = lax.rem(me, GROUP), me // GROUP
    z, core = j // 2, lax.rem(j, 2)
    y, x = g // 4, lax.rem(g, 4)
    z_peers = [lax.rem(z + dz, 8) * 2 + lax.rem(core + dc, 2) for dz, dc in ALONG_Z]
    xy_peers = [lax.rem(y + dy, 4) * 4 + lax.rem(x + dx, 4) for dy, dx in ACROSS]

    barrier = pltpu.get_barrier_semaphore()
    for peer in z_peers:
        pl.semaphore_signal(barrier, inc=1, device_id=(g * GROUP + peer,), device_id_type=MESH)
    for peer in xy_peers:
        pl.semaphore_signal(barrier, inc=1, device_id=(peer * GROUP + j,), device_id_type=MESH)

    load = pltpu.make_async_copy(signal_hbm, signal, load_sem)
    load.start()
    weights = [
        pltpu.make_async_copy(conv_hbm, conv, weight_sem.at[0]),
        pltpu.make_async_copy(res_hbm, proj.at[:, :, pl.ds(0, C)], weight_sem.at[1]),
        pltpu.make_async_copy(skip_hbm, proj.at[:, :, pl.ds(C, C)], weight_sem.at[2]),
    ]
    for copy in weights:
        copy.start()
    swap256[...] = one_hot(256, lambda o: (o & 15) * 16 + (o >> 4))
    split512[...] = one_hot(LENGTH, lambda o: (o & 31) * 16 + (o >> 5))
    join512[...] = one_hot(LENGTH, lambda o: (o & 15) * 32 + (o >> 4))
    turn512[...] = one_hot(LENGTH, lambda o: ((o >> 1) & 15) * 32 + (o >> 5) * 2 + (o & 1))
    enter512[...] = one_hot(
        LENGTH,
        lambda o: jnp.where(
            (o & 1) == 0, ((o >> 1) & 15) * 16 + (o >> 5), 256 + (o >> 5) * 16 + ((o >> 1) & 15)
        ),
    )
    cur[pl.ds(0, PAD), :] = jnp.zeros((PAD, C), F32)
    cur[pl.ds(PAD + LENGTH, PAD), :] = jnp.zeros((PAD, C), F32)
    load.wait()
    slab = (GROUP, 16, C)
    sent_xy[...] = signal[0, pl.ds(0, 256), :].astype(BF16).reshape(slab)
    swap = swap256[...]
    sent_z[...] = reordered(swap, signal[1, pl.ds(0, 256), :].astype(BF16)).astype(BF16).reshape(slab)
    for half in range(HALVES):
        rows = reordered(swap, signal[half, pl.ds(256, 256), :].astype(BF16))
        sent_late[:, half] = rows.astype(BF16).reshape(slab)
    pl.semaphore_wait(barrier, 2 * (GROUP - 1))

    started = []

    def send(src, dst, peer, along_z, stage):
        device = g * GROUP + peer if along_z else peer * GROUP + j
        pltpu.make_async_remote_copy(
            src_ref=src,
            dst_ref=dst,
            send_sem=send_sem.at[stage],
            recv_sem=recv_sem.at[stage],
            device_id=(device,),
            device_id_type=MESH,
        ).start()

    def exchange(source, target, along_z, stage):
        mine = j if along_z else g
        for peer in z_peers if along_z else xy_peers:
            send(source.at[peer], target.at[mine], peer, along_z, stage)
        target[mine] = source[mine]
        started.append((source, stage))

    def finish(source, sem):
        part = source.at[pl.ds(0, GROUP - 1)]
        pltpu.make_async_copy(part, part, sem).wait()

    def wait_for(target, stage):
        finish(target, recv_sem.at[stage])

    exchange(sent_xy, first_xy, False, 0)
    exchange(sent_z, first_z, True, 1)
    wait_for(first_xy, 0)
    next_z[...] = reordered(swap256[...], first_xy[...].reshape(256, C)).astype(BF16).reshape(slab)
    exchange(next_z, halves.at[0], True, 2)
    exchange(sent_late, late_z, True, 3)
    wait_for(first_z, 1)
    next_xy[...] = reordered(swap256[...], first_z[...].reshape(256, C)).astype(BF16).reshape(slab)
    exchange(next_xy, halves.at[1], False, 4)

    def layers():
        for layer in range(LAYERS):
            d = 2**layer
            for tap in range(3):
                x3[:, pl.ds(tap * C, C)] = cur[pl.ds(PAD + (tap - 1) * d, LENGTH), :].astype(BF16)
            for tile in range(LENGTH // TILE):
                at = pl.ds(tile * TILE, TILE)
                at_cur = pl.ds(PAD + tile * TILE, TILE)
                pre = jnp.dot(x3[at, :], conv[layer], preferred_element_type=F32)
                pre = pre + bias_ref[pl.ds(layer, 1), :]
                gated = (jnp.tanh(pre[:, :C]) * (0.5 + 0.5 * jnp.tanh(0.5 * pre[:, C:]))).astype(BF16)
                both = jnp.dot(gated, proj[layer], preferred_element_type=F32)
                if layer < LAYERS - 1:
                    cur[at_cur, :] = cur[at_cur, :] + both[:, :C]
                    skip[at, :] = both[:, C:] if layer == 0 else skip[at, :] + both[:, C:]
                else:
                    delta = (cur[at_cur, :] - start[at, :].astype(F32)) + both[:, :C]
                    result[0, at, :] = delta.astype(BF16)
                    result[1, at, :] = (skip[at, :] + both[:, C:]).astype(BF16)

    wide = (GROUP, 32, C)

    def leave_along_z(unit, part, stage):
        rows = reordered(turn512[...], result[part])
        leave[unit] = rows.astype(BF16).reshape(wide)
        exchange(leave.at[unit], passing.at[unit], True, stage)

    own = []

    def last_stage(unit, out, chunk, along_z, arrival, stage):
        wait_for(passing.at[unit], arrival)
        rows = reordered(join512[...], passing[unit].reshape(LENGTH, C))
        last[unit] = rows.astype(BF16).reshape(GROUP, HALVES, 16, C)
        mine = j if along_z else g
        owner = j if along_z else g
        at = pl.ds(pl.multiple_of(chunk * 256 + owner * 16, 16), 16)
        for peer in z_peers if along_z else xy_peers:
            send(last.at[unit, peer], out.at[:, at, :], peer, along_z, stage)
        copy = pltpu.make_async_copy(last.at[unit, mine], out.at[:, at, :], own_sem.at[unit])
        copy.start()
        own.append(copy)
        started.append((last.at[unit], stage))

    for copy in weights:
        copy.wait()
    wait_for(halves.at[0], 2)
    wait_for(halves.at[1], 4)
    rows = reordered(enter512[...], halves[...].reshape(LENGTH, C))
    cur[pl.ds(PAD, LENGTH), :] = rows
    start[...] = rows.astype(BF16)
    layers()
    leave_along_z(0, 0, 6)
    leave_along_z(1, 1, 7)

    wait_for(late_z, 3)
    rows = reordered(split512[...], late_z[...].reshape(LENGTH, C))
    late_next[...] = rows.astype(BF16).reshape(wide)
    exchange(late_next, late, False, 5)
    wait_for(late, 5)
    start[...] = late[...].reshape(LENGTH, C)
    cur[pl.ds(PAD, LENGTH), :] = start[...].astype(F32)
    layers()
    leave[3] = result[1].reshape(wide)
    exchange(leave.at[3], passing.at[3], False, 9)
    leave_along_z(2, 0, 8)

    last_stage(0, delta_out, 0, False, 6, 10)
    last_stage(1, skip_out, 0, False, 7, 11)
    last_stage(3, skip_out, 1, True, 9, 13)
    last_stage(2, delta_out, 1, False, 8, 12)

    for unit, stage in ((0, 10), (1, 11), (3, 13), (2, 12)):
        wait_for(last.at[unit], stage)
    for copy in own:
        copy.wait()
    for source, stage in started:
        finish(source, send_sem.at[stage])


def finish_kernel(signal_ref, delta_ref, skip_in_ref, features_ref, skip_ref):
    features_ref[...] = signal_ref[...] + delta_ref[...].astype(F32)
    chunk = lax.rem(pl.program_id(0), 2)

    @pl.when(chunk == 0)
    def _():
        skip_ref[...] = skip_in_ref[...].astype(F32)

    @pl.when(chunk == 1)
    def _():
        swap = one_hot(256, lambda o: (o & 15) * 16 + (o >> 4))
        skip_ref[...] = reordered(swap, skip_in_ref[...])


def body(signal, conv_weight, conv_bias, res_weight, skip_weight):
    any_space = pl.BlockSpec(memory_space=pl.ANY)

    def vmem(*shape, dtype=BF16):
        return pltpu.VMEM(shape, dtype)

    delta, skip_sum = pl.pallas_call(
        kernel,
        out_shape=[jax.ShapeDtypeStruct((HALVES, RESIDUES, C), BF16)] * 2,
        in_specs=[any_space, any_space, pl.BlockSpec(memory_space=pltpu.VMEM), any_space, any_space],
        out_specs=[any_space, any_space],
        scratch_shapes=[
            vmem(HALVES, RESIDUES, C, dtype=F32),
            vmem(LAYERS, 3 * C, 2 * C),
            vmem(LAYERS, C, 2 * C),
            vmem(256, 256),
            vmem(LENGTH, LENGTH),
            vmem(LENGTH, LENGTH),
            vmem(LENGTH, LENGTH),
            vmem(LENGTH, LENGTH),
            vmem(GROUP, 16, C),
            vmem(GROUP, 16, C),
            vmem(GROUP, HALVES, 16, C),
            vmem(GROUP, 16, C),
            vmem(GROUP, 16, C),
            vmem(GROUP, 16, C),
            vmem(GROUP, 16, C),
            vmem(2, GROUP, 16, C),
            vmem(GROUP, HALVES, 16, C),
            vmem(GROUP, 32, C),
            vmem(GROUP, 32, C),
            vmem(4, GROUP, 32, C),
            vmem(4, GROUP, 32, C),
            vmem(4, GROUP, HALVES, 16, C),
            vmem(LENGTH + 2 * PAD, C, dtype=F32),
            vmem(LENGTH, C, dtype=F32),
            vmem(LENGTH, C),
            vmem(2, LENGTH, C),
            vmem(LENGTH, 3 * C),
            pltpu.SemaphoreType.DMA,
            pltpu.SemaphoreType.DMA((3,)),
            pltpu.SemaphoreType.DMA((14,)),
            pltpu.SemaphoreType.DMA((14,)),
            pltpu.SemaphoreType.DMA((4,)),
        ],
        compiler_params=pltpu.CompilerParams(
            collective_id=0, has_side_effects=True, vmem_limit_bytes=60 * 2**20
        ),
    )(
        signal.reshape(HALVES, RESIDUES, C),
        conv_weight,
        conv_bias,
        res_weight,
        skip_weight,
    )
    block = pl.BlockSpec((256, C), lambda i: (i, 0))
    shape = signal.shape
    return pl.pallas_call(
        finish_kernel,
        grid=(shape[0] // 256,),
        out_shape=[jax.ShapeDtypeStruct(shape, F32)] * 2,
        in_specs=[block, block, block],
        out_specs=[block, block],
    )(signal, delta.reshape(shape), skip_sum.reshape(shape))


def solution(mesh):
    in_specs = (P("seq", None), P(), P(), P(), P())
    out_specs = (P("seq", None), P("seq", None))
    return jax.shard_map(body, mesh=mesh, in_specs=in_specs, out_specs=out_specs, check_vma=False)
```

time: 76.6 us -> 65.2 us (0.85)
  Pallas kernels: 71.6 us -> 64.4 us
  other arithmetic: 4.2 us -> 0 us
    pallas_call x1, Pallas kernels: 71.6 us -> 60.4 us  [body(): pl.pallas_call(kernel, out_shape=[jax.ShapeDtypeStruct((HALVES, RESIDUES,...]
    pallas_call x0 -> x1, Pallas kernels: none -> 3.95 us  [body(): pl.pallas_call(finish_kernel, grid=(shape[0] // 256,), out_shape=[jax.Sha...]
    add x1 -> x0, other arithmetic: 2.11 us -> none  [body(): signal + delta.reshape(shape).astype(F32)]
    convert_element_type x1 -> x0, other arithmetic: 2.09 us -> none  [body(): skip_sum.reshape(shape).astype(F32)]
where the time goes in v3:
time: 65.2 us; the launch traced here: 65 us
  Pallas kernels  64.4 us (99%)
    pallas_call x1, Pallas kernels, body(): pl.pallas_call(kernel, out_shape=[jax.ShapeDtypeStruct((HALVES, RESIDUES,...  60.4 us
    pallas_call x1, Pallas kernels, body(): pl.pallas_call(finish_kernel, grid=(shape[0] // 256,), out_shape=[jax.Sha...  3.95 us

profile of v3, /device:TPU:1, one launch (start us, length us, event | category | flops | bytes accessed | tf_op | source)
XLA Modules:
  0.0 65.0 jit_solution(10480966722055133364)
XLA Ops:
  0.6 60.4 %shard_map.68 = (bf16[2,512,256]{2,1,0:T(8,128)(2,1)}, bf16[2,512,256]{2,1,0:T(8,128)(2,1)}) custom-call(f32[2,512,256]{2,1,0:T(8,128)} %bitcast.3, bf16[6,768,512]{2,1,0:T(8,128)(2,1)} %conv_hbm.1, f32[6,512]{1,0:T(8,128)} %bias_ref.1, bf16[6,256,256]{2,1,0:T(8,128)(2,1)} %res_hbm.1, bf16[6,256,256]{2,1,0:T(8,128)(2,1)} %skip_hbm.1), custom_call_target="tpu_custom_call" | custom-call | tf_op jit(solution)/shard_map/pallas_call | solution.py:255
  61.1 4.0 %shard_map.69 = (f32[1024,256]{1,0:T(8,128)}, f32[1024,256]{1,0:T(8,128)}) custom-call(f32[1024,256]{1,0:T(8,128)} %signal_ref.1, bf16[1024,256]{1,0:T(8,128)(2,1)} %bitcast.4, bf16[1024,256]{1,0:T(8,128)(2,1)} %bitcast.5), custom_call_target="tpu_custom_call" | custom-call | tf_op jit(solution)/shard_map/pallas_call | solution.py:306

commit v4 on v3

--- a/solution.py
+++ b/solution.py
@@ -12,7 +12,6 @@
 LENGTH = 512
 C = 256
 PAD = 32
-TILE = 256
 MESH = pl.DeviceIdType.MESH
 BF16 = jnp.bfloat16
 F32 = jnp.float32
@@ -114,9 +113,14 @@
     for half in range(HALVES):
         rows = reordered(swap, signal[half, pl.ds(256, 256), :].astype(BF16))
         sent_late[:, half] = rows.astype(BF16).reshape(slab)
+    for copy in weights:
+        copy.wait()
+    for layer in range(LAYERS):
+        conv[layer, :, pl.ds(C, C)] = conv[layer, :, pl.ds(C, C)] * jnp.asarray(0.5, BF16)
+        proj[layer] = proj[layer] * jnp.asarray(0.5, BF16)
     pl.semaphore_wait(barrier, 2 * (GROUP - 1))
 
-    started = []
+    started = {}
 
     def send(src, dst, peer, along_z, stage):
         device = g * GROUP + peer if along_z else peer * GROUP + j
@@ -134,7 +138,7 @@
         for peer in z_peers if along_z else xy_peers:
             send(source.at[peer], target.at[mine], peer, along_z, stage)
         target[mine] = source[mine]
-        started.append((source, stage))
+        started[stage] = source
 
     def finish(source, sem):
         part = source.at[pl.ds(0, GROUP - 1)]
@@ -158,20 +162,19 @@
             d = 2**layer
             for tap in range(3):
                 x3[:, pl.ds(tap * C, C)] = cur[pl.ds(PAD + (tap - 1) * d, LENGTH), :].astype(BF16)
-            for tile in range(LENGTH // TILE):
-                at = pl.ds(tile * TILE, TILE)
-                at_cur = pl.ds(PAD + tile * TILE, TILE)
-                pre = jnp.dot(x3[at, :], conv[layer], preferred_element_type=F32)
-                pre = pre + bias_ref[pl.ds(layer, 1), :]
-                gated = (jnp.tanh(pre[:, :C]) * (0.5 + 0.5 * jnp.tanh(0.5 * pre[:, C:]))).astype(BF16)
-                both = jnp.dot(gated, proj[layer], preferred_element_type=F32)
-                if layer < LAYERS - 1:
-                    cur[at_cur, :] = cur[at_cur, :] + both[:, :C]
-                    skip[at, :] = both[:, C:] if layer == 0 else skip[at, :] + both[:, C:]
-                else:
-                    delta = (cur[at_cur, :] - start[at, :].astype(F32)) + both[:, :C]
-                    result[0, at, :] = delta.astype(BF16)
-                    result[1, at, :] = (skip[at, :] + both[:, C:]).astype(BF16)
+            pre = jnp.dot(x3[...], conv[layer], preferred_element_type=F32)
+            filtered = jnp.tanh(pre[:, :C] + bias_ref[pl.ds(layer, 1), pl.ds(0, C)])
+            gate = jnp.tanh(pre[:, C:] + 0.5 * bias_ref[pl.ds(layer, 1), pl.ds(C, C)])
+            twice_gated = (filtered + filtered * gate).astype(BF16)
+            both = jnp.dot(twice_gated, proj[layer], preferred_element_type=F32)
+            at_cur = pl.ds(PAD, LENGTH)
+            if layer < LAYERS - 1:
+                cur[at_cur, :] = cur[at_cur, :] + both[:, :C]
+                skip[...] = both[:, C:] if layer == 0 else skip[...] + both[:, C:]
+            else:
+                delta = (cur[at_cur, :] - start[...].astype(F32)) + both[:, :C]
+                result[0] = delta.astype(BF16)
+                result[1] = (skip[...] + both[:, C:]).astype(BF16)
 
     wide = (GROUP, 32, C)
 
@@ -194,10 +197,8 @@
         copy = pltpu.make_async_copy(last.at[unit, mine], out.at[:, at, :], own_sem.at[unit])
         copy.start()
         own.append(copy)
-        started.append((last.at[unit], stage))
-
-    for copy in weights:
-        copy.wait()
+        started[stage] = last.at[unit]
+
     wait_for(halves.at[0], 2)
     wait_for(halves.at[1], 4)
     rows = reordered(enter512[...], halves[...].reshape(LENGTH, C))
@@ -205,12 +206,12 @@
     start[...] = rows.astype(BF16)
     layers()
     leave_along_z(0, 0, 6)
-    leave_along_z(1, 1, 7)
 
     wait_for(late_z, 3)
     rows = reordered(split512[...], late_z[...].reshape(LENGTH, C))
     late_next[...] = rows.astype(BF16).reshape(wide)
     exchange(late_next, late, False, 5)
+    leave_along_z(1, 1, 7)
     wait_for(late, 5)
     start[...] = late[...].reshape(LENGTH, C)
     cur[pl.ds(PAD, LENGTH), :] = start[...].astype(F32)
@@ -221,6 +222,8 @@
 
     last_stage(0, delta_out, 0, False, 6, 10)
     last_stage(1, skip_out, 0, False, 7, 11)
+    finish(leave.at[2], send_sem.at[8])
+    del started[8]
     last_stage(3, skip_out, 1, True, 9, 13)
     last_stage(2, delta_out, 1, False, 8, 12)
 
@@ -228,22 +231,16 @@
         wait_for(last.at[unit], stage)
     for copy in own:
         copy.wait()
-    for source, stage in started:
+    for stage, source in started.items():
         finish(source, send_sem.at[stage])
 
 
 def finish_kernel(signal_ref, delta_ref, skip_in_ref, features_ref, skip_ref):
     features_ref[...] = signal_ref[...] + delta_ref[...].astype(F32)
-    chunk = lax.rem(pl.program_id(0), 2)
-
-    @pl.when(chunk == 0)
-    def _():
-        skip_ref[...] = skip_in_ref[...].astype(F32)
-
-    @pl.when(chunk == 1)
-    def _():
-        swap = one_hot(256, lambda o: (o & 15) * 16 + (o >> 4))
-        skip_ref[...] = reordered(swap, skip_in_ref[...])
+    first, second = pl.ds(0, 256), pl.ds(256, 256)
+    skip_ref[first, :] = skip_in_ref[first, :].astype(F32)
+    swap = one_hot(256, lambda o: (o & 15) * 16 + (o >> 4))
+    skip_ref[second, :] = reordered(swap, skip_in_ref[second, :])
 
 
 def body(signal, conv_weight, conv_bias, res_weight, skip_weight):
@@ -301,11 +298,11 @@
         res_weight,
         skip_weight,
     )
-    block = pl.BlockSpec((256, C), lambda i: (i, 0))
+    block = pl.BlockSpec((RESIDUES, C), lambda i: (i, 0))
     shape = signal.shape
     return pl.pallas_call(
         finish_kernel,
-        grid=(shape[0] // 256,),
+        grid=(HALVES,),
         out_shape=[jax.ShapeDtypeStruct(shape, F32)] * 2,
         in_specs=[block, block, block],
         out_specs=[block, block],

time: 65.2 us -> 60.4 us (0.926)
  Pallas kernels: 64.4 us -> 59.6 us
    pallas_call x1, Pallas kernels: 60.4 us -> 56.9 us  [body(): pl.pallas_call(kernel, out_shape=[jax.ShapeDtypeStruct((HALVES, RESIDUES,...]
    pallas_call x1, Pallas kernels: 3.95 us -> 2.7 us  [body(): pl.pallas_call(finish_kernel, grid=(HALVES,), out_shape=[jax.ShapeDtypeSt...]
where the time goes in v4:
time: 60.4 us; the launch traced here: 60.3 us
  Pallas kernels  59.6 us (99%)
  between operations  0.64 us (1%)
    pallas_call x1, Pallas kernels, body(): pl.pallas_call(kernel, out_shape=[jax.ShapeDtypeStruct((HALVES, RESIDUES,...  56.9 us
    pallas_call x1, Pallas kernels, body(): pl.pallas_call(finish_kernel, grid=(HALVES,), out_shape=[jax.ShapeDtypeSt...  2.7 us

profile of v4, /device:TPU:1, one launch (start us, length us, event | category | flops | bytes accessed | tf_op | source)
XLA Modules:
  0.0 60.3 jit_solution(7997319403003234086)
XLA Ops:
  0.6 56.9 %shard_map.68 = (bf16[2,512,256]{2,1,0:T(8,128)(2,1)}, bf16[2,512,256]{2,1,0:T(8,128)(2,1)}) custom-call(f32[2,512,256]{2,1,0:T(8,128)} %bitcast.3, bf16[6,768,512]{2,1,0:T(8,128)(2,1)} %conv_hbm.1, f32[6,512]{1,0:T(8,128)} %bias_ref.1, bf16[6,256,256]{2,1,0:T(8,128)(2,1)} %res_hbm.1, bf16[6,256,256]{2,1,0:T(8,128)(2,1)} %skip_hbm.1), custom_call_target="tpu_custom_call" | custom-call | tf_op jit(solution)/shard_map/pallas_call | solution.py:252
  57.6 2.7 %shard_map.69 = (f32[1024,256]{1,0:T(8,128)}, f32[1024,256]{1,0:T(8,128)}) custom-call(f32[1024,256]{1,0:T(8,128)} %signal_ref.1, bf16[1024,256]{1,0:T(8,128)(2,1)} %bitcast.4, bf16[1024,256]{1,0:T(8,128)(2,1)} %bitcast.5), custom_call_target="tpu_custom_call" | custom-call | tf_op jit(solution)/shard_map/pallas_call | solution.py:303

commit v5 on v4

--- a/solution.py
+++ b/solution.py
@@ -40,7 +40,8 @@
     skip_out,
     signal,
     conv,
-    proj,
+    res_proj,
+    skip_proj,
     swap256,
     split512,
     join512,
@@ -61,7 +62,7 @@
     passing,
     last,
     cur,
-    skip,
+    all_gated,
     start,
     result,
     x3,
@@ -88,8 +89,8 @@
     load.start()
     weights = [
         pltpu.make_async_copy(conv_hbm, conv, weight_sem.at[0]),
-        pltpu.make_async_copy(res_hbm, proj.at[:, :, pl.ds(0, C)], weight_sem.at[1]),
-        pltpu.make_async_copy(skip_hbm, proj.at[:, :, pl.ds(C, C)], weight_sem.at[2]),
+        pltpu.make_async_copy(res_hbm, res_proj, weight_sem.at[1]),
+        pltpu.make_async_copy(skip_hbm, skip_proj, weight_sem.at[2]),
     ]
     for copy in weights:
         copy.start()
@@ -117,7 +118,9 @@
         copy.wait()
     for layer in range(LAYERS):
         conv[layer, :, pl.ds(C, C)] = conv[layer, :, pl.ds(C, C)] * jnp.asarray(0.5, BF16)
-        proj[layer] = proj[layer] * jnp.asarray(0.5, BF16)
+        res_proj[layer] = res_proj[layer] * jnp.asarray(0.5, BF16)
+        at = pl.ds(layer * C, C)
+        skip_proj[at, :] = skip_proj[at, :] * jnp.asarray(0.5, BF16)
     pl.semaphore_wait(barrier, 2 * (GROUP - 1))
 
     started = {}
@@ -152,10 +155,12 @@
     wait_for(first_xy, 0)
     next_z[...] = reordered(swap256[...], first_xy[...].reshape(256, C)).astype(BF16).reshape(slab)
     exchange(next_z, halves.at[0], True, 2)
-    exchange(sent_late, late_z, True, 3)
     wait_for(first_z, 1)
     next_xy[...] = reordered(swap256[...], first_z[...].reshape(256, C)).astype(BF16).reshape(slab)
     exchange(next_xy, halves.at[1], False, 4)
+    finish(next_z, send_sem.at[2])
+    del started[2]
+    exchange(sent_late, late_z, True, 3)
 
     def layers():
         for layer in range(LAYERS):
@@ -166,15 +171,17 @@
             filtered = jnp.tanh(pre[:, :C] + bias_ref[pl.ds(layer, 1), pl.ds(0, C)])
             gate = jnp.tanh(pre[:, C:] + 0.5 * bias_ref[pl.ds(layer, 1), pl.ds(C, C)])
             twice_gated = (filtered + filtered * gate).astype(BF16)
-            both = jnp.dot(twice_gated, proj[layer], preferred_element_type=F32)
+            all_gated[:, pl.ds(layer * C, C)] = twice_gated
+            added = jnp.dot(twice_gated, res_proj[layer], preferred_element_type=F32)
             at_cur = pl.ds(PAD, LENGTH)
             if layer < LAYERS - 1:
-                cur[at_cur, :] = cur[at_cur, :] + both[:, :C]
-                skip[...] = both[:, C:] if layer == 0 else skip[...] + both[:, C:]
+                cur[at_cur, :] = cur[at_cur, :] + added
             else:
-                delta = (cur[at_cur, :] - start[...].astype(F32)) + both[:, :C]
-                result[0] = delta.astype(BF16)
-                result[1] = (skip[...] + both[:, C:]).astype(BF16)
+                result[0] = ((cur[at_cur, :] - start[...].astype(F32)) + added).astype(BF16)
+
+    def skip_sums():
+        sums = jnp.dot(all_gated[...], skip_proj[...], preferred_element_type=F32)
+        result[1] = sums.astype(BF16)
 
     wide = (GROUP, 32, C)
 
@@ -206,28 +213,30 @@
     start[...] = rows.astype(BF16)
     layers()
     leave_along_z(0, 0, 6)
+    skip_sums()
+    leave_along_z(1, 1, 7)
 
     wait_for(late_z, 3)
     rows = reordered(split512[...], late_z[...].reshape(LENGTH, C))
     late_next[...] = rows.astype(BF16).reshape(wide)
     exchange(late_next, late, False, 5)
-    leave_along_z(1, 1, 7)
     wait_for(late, 5)
     start[...] = late[...].reshape(LENGTH, C)
     cur[pl.ds(PAD, LENGTH), :] = start[...].astype(F32)
     layers()
-    leave[3] = result[1].reshape(wide)
-    exchange(leave.at[3], passing.at[3], False, 9)
-    leave_along_z(2, 0, 8)
+    leave[2] = result[0].reshape(wide)
+    exchange(leave.at[2], passing.at[2], False, 8)
+    skip_sums()
+    leave_along_z(3, 1, 9)
 
     last_stage(0, delta_out, 0, False, 6, 10)
     last_stage(1, skip_out, 0, False, 7, 11)
-    finish(leave.at[2], send_sem.at[8])
-    del started[8]
-    last_stage(3, skip_out, 1, True, 9, 13)
-    last_stage(2, delta_out, 1, False, 8, 12)
-
-    for unit, stage in ((0, 10), (1, 11), (3, 13), (2, 12)):
+    finish(leave.at[3], send_sem.at[9])
+    del started[9]
+    last_stage(2, delta_out, 1, True, 8, 12)
+    last_stage(3, skip_out, 1, False, 9, 13)
+
+    for unit, stage in ((0, 10), (1, 11), (2, 12), (3, 13)):
         wait_for(last.at[unit], stage)
     for copy in own:
         copy.wait()
@@ -236,11 +245,11 @@
 
 
 def finish_kernel(signal_ref, delta_ref, skip_in_ref, features_ref, skip_ref):
-    features_ref[...] = signal_ref[...] + delta_ref[...].astype(F32)
+    skip_ref[...] = skip_in_ref[...].astype(F32)
     first, second = pl.ds(0, 256), pl.ds(256, 256)
-    skip_ref[first, :] = skip_in_ref[first, :].astype(F32)
+    features_ref[first, :] = signal_ref[first, :] + delta_ref[first, :].astype(F32)
     swap = one_hot(256, lambda o: (o & 15) * 16 + (o >> 4))
-    skip_ref[second, :] = reordered(swap, skip_in_ref[second, :])
+    features_ref[second, :] = signal_ref[second, :] + reordered(swap, delta_ref[second, :])
 
 
 def body(signal, conv_weight, conv_bias, res_weight, skip_weight):
@@ -257,7 +266,8 @@
         scratch_shapes=[
             vmem(HALVES, RESIDUES, C, dtype=F32),
             vmem(LAYERS, 3 * C, 2 * C),
-            vmem(LAYERS, C, 2 * C),
+            vmem(LAYERS, C, C),
+            vmem(LAYERS * C, C),
             vmem(256, 256),
             vmem(LENGTH, LENGTH),
             vmem(LENGTH, LENGTH),
@@ -278,7 +288,7 @@
             vmem(4, GROUP, 32, C),
             vmem(4, GROUP, HALVES, 16, C),
             vmem(LENGTH + 2 * PAD, C, dtype=F32),
-            vmem(LENGTH, C, dtype=F32),
+            vmem(LENGTH, LAYERS * C),
             vmem(LENGTH, C),
             vmem(2, LENGTH, C),
             vmem(LENGTH, 3 * C),
@@ -296,7 +306,7 @@
         conv_weight,
         conv_bias,
         res_weight,
-        skip_weight,
+        skip_weight.reshape(LAYERS * C, C),
     )
     block = pl.BlockSpec((RESIDUES, C), lambda i: (i, 0))
     shape = signal.shape

time: 60.4 us -> 62.4 us (1.033)
  Pallas kernels: 59.6 us -> 61.6 us
    pallas_call x1, Pallas kernels: 56.9 us -> 58.9 us  [body(): pl.pallas_call(kernel, out_shape=[jax.ShapeDtypeStruct((HALVES, RESIDUES,...]
where the time goes in v5:
time: 62.4 us; the launch traced here: 62.2 us
  Pallas kernels  61.6 us (99%)
  between operations  0.64 us (1%)
    pallas_call x1, Pallas kernels, body(): pl.pallas_call(kernel, out_shape=[jax.ShapeDtypeStruct((HALVES, RESIDUES,...  58.9 us
    pallas_call x1, Pallas kernels, body(): pl.pallas_call(finish_kernel, grid=(HALVES,), out_shape=[jax.ShapeDtypeSt...  2.69 us

profile of v5, /device:TPU:1, one launch (start us, length us, event | category | flops | bytes accessed | tf_op | source)
XLA Modules:
  0.0 62.2 jit_solution(12330818840462154755)
XLA Ops:
  0.6 58.9 %shard_map.68 = (bf16[2,512,256]{2,1,0:T(8,128)(2,1)}, bf16[2,512,256]{2,1,0:T(8,128)(2,1)}) custom-call(f32[2,512,256]{2,1,0:T(8,128)} %bitcast.4, bf16[6,768,512]{2,1,0:T(8,128)(2,1)} %conv_hbm.1, f32[6,512]{1,0:T(8,128)} %bias_ref.1, bf16[6,256,256]{2,1,0:T(8,128)(2,1)} %res_hbm.1, bf16[1536,256]{1,0:T(8,128)(2,1)} %bitcast.5), custom_call_target="tpu_custom_call" | custom-call | tf_op jit(solution)/shard_map/pallas_call | solution.py:261
  59.5 2.7 %shard_map.69 = (f32[1024,256]{1,0:T(8,128)}, f32[1024,256]{1,0:T(8,128)}) custom-call(f32[1024,256]{1,0:T(8,128)} %signal_ref.1, bf16[1024,256]{1,0:T(8,128)(2,1)} %bitcast.6, bf16[1024,256]{1,0:T(8,128)(2,1)} %bitcast.7), custom_call_target="tpu_custom_call" | custom-call | tf_op jit(solution)/shard_map/pallas_call | solution.py:313

commit v6 on v5

--- a/solution.py
+++ b/solution.py
@@ -55,7 +55,7 @@
     next_z,
     next_xy,
     halves,
-    late_z,
+    late_first,
     late_next,
     late,
     leave,
@@ -109,11 +109,9 @@
     load.wait()
     slab = (GROUP, 16, C)
     sent_xy[...] = signal[0, pl.ds(0, 256), :].astype(BF16).reshape(slab)
-    swap = swap256[...]
-    sent_z[...] = reordered(swap, signal[1, pl.ds(0, 256), :].astype(BF16)).astype(BF16).reshape(slab)
+    sent_z[...] = reordered(swap256[...], signal[1, pl.ds(0, 256), :].astype(BF16)).astype(BF16).reshape(slab)
     for half in range(HALVES):
-        rows = reordered(swap, signal[half, pl.ds(256, 256), :].astype(BF16))
-        sent_late[:, half] = rows.astype(BF16).reshape(slab)
+        sent_late[:, half] = signal[half, pl.ds(256, 256), :].astype(BF16).reshape(slab)
     for copy in weights:
         copy.wait()
     for layer in range(LAYERS):
@@ -152,15 +150,17 @@
 
     exchange(sent_xy, first_xy, False, 0)
     exchange(sent_z, first_z, True, 1)
+    exchange(sent_late, late_first, False, 3)
     wait_for(first_xy, 0)
     next_z[...] = reordered(swap256[...], first_xy[...].reshape(256, C)).astype(BF16).reshape(slab)
     exchange(next_z, halves.at[0], True, 2)
     wait_for(first_z, 1)
     next_xy[...] = reordered(swap256[...], first_z[...].reshape(256, C)).astype(BF16).reshape(slab)
     exchange(next_xy, halves.at[1], False, 4)
-    finish(next_z, send_sem.at[2])
-    del started[2]
-    exchange(sent_late, late_z, True, 3)
+    wait_for(late_first, 3)
+    rows = reordered(split512[...], late_first[...].reshape(LENGTH, C))
+    late_next[...] = rows.astype(BF16).reshape(GROUP, 32, C)
+    exchange(late_next, late, True, 5)
 
     def layers():
         for layer in range(LAYERS):
@@ -216,25 +216,21 @@
     skip_sums()
     leave_along_z(1, 1, 7)
 
-    wait_for(late_z, 3)
-    rows = reordered(split512[...], late_z[...].reshape(LENGTH, C))
-    late_next[...] = rows.astype(BF16).reshape(wide)
-    exchange(late_next, late, False, 5)
     wait_for(late, 5)
-    start[...] = late[...].reshape(LENGTH, C)
-    cur[pl.ds(PAD, LENGTH), :] = start[...].astype(F32)
+    rows = reordered(turn512[...], late[...].reshape(LENGTH, C))
+    cur[pl.ds(PAD, LENGTH), :] = rows
+    start[...] = rows.astype(BF16)
     layers()
     leave[2] = result[0].reshape(wide)
     exchange(leave.at[2], passing.at[2], False, 8)
     skip_sums()
-    leave_along_z(3, 1, 9)
-
+    leave[3] = result[1].reshape(wide)
+    exchange(leave.at[3], passing.at[3], False, 9)
+
+    last_stage(2, delta_out, 1, True, 8, 12)
+    last_stage(3, skip_out, 1, True, 9, 13)
     last_stage(0, delta_out, 0, False, 6, 10)
     last_stage(1, skip_out, 0, False, 7, 11)
-    finish(leave.at[3], send_sem.at[9])
-    del started[9]
-    last_stage(2, delta_out, 1, True, 8, 12)
-    last_stage(3, skip_out, 1, False, 9, 13)
 
     for unit, stage in ((0, 10), (1, 11), (2, 12), (3, 13)):
         wait_for(last.at[unit], stage)
@@ -245,11 +241,12 @@
 
 
 def finish_kernel(signal_ref, delta_ref, skip_in_ref, features_ref, skip_ref):
-    skip_ref[...] = skip_in_ref[...].astype(F32)
     first, second = pl.ds(0, 256), pl.ds(256, 256)
     features_ref[first, :] = signal_ref[first, :] + delta_ref[first, :].astype(F32)
+    skip_ref[first, :] = skip_in_ref[first, :].astype(F32)
     swap = one_hot(256, lambda o: (o & 15) * 16 + (o >> 4))
     features_ref[second, :] = signal_ref[second, :] + reordered(swap, delta_ref[second, :])
+    skip_ref[second, :] = reordered(swap, skip_in_ref[second, :])
 
 
 def body(signal, conv_weight, conv_bias, res_weight, skip_weight):

time: 62.4 us -> 57.8 us (0.926)
  Pallas kernels: 61.6 us -> 57 us
    pallas_call x1, Pallas kernels: 58.9 us -> 54.3 us  [body(): pl.pallas_call(kernel, out_shape=[jax.ShapeDtypeStruct((HALVES, RESIDUES,...]
where the time goes in v6:
time: 57.8 us; the launch traced here: 57.7 us
  Pallas kernels  57 us (99%)
  between operations  0.64 us (1%)
    pallas_call x1, Pallas kernels, body(): pl.pallas_call(kernel, out_shape=[jax.ShapeDtypeStruct((HALVES, RESIDUES,...  54.3 us
    pallas_call x1, Pallas kernels, body(): pl.pallas_call(finish_kernel, grid=(HALVES,), out_shape=[jax.ShapeDtypeSt...  2.75 us

profile of v6, /device:TPU:1, one launch (start us, length us, event | category | flops | bytes accessed | tf_op | source)
XLA Modules:
  0.0 57.7 jit_solution(14356674831869186494)
XLA Ops:
  0.6 54.3 %shard_map.68 = (bf16[2,512,256]{2,1,0:T(8,128)(2,1)}, bf16[2,512,256]{2,1,0:T(8,128)(2,1)}) custom-call(f32[2,512,256]{2,1,0:T(8,128)} %bitcast.4, bf16[6,768,512]{2,1,0:T(8,128)(2,1)} %conv_hbm.1, f32[6,512]{1,0:T(8,128)} %bias_ref.1, bf16[6,256,256]{2,1,0:T(8,128)(2,1)} %res_hbm.1, bf16[1536,256]{1,0:T(8,128)(2,1)} %bitcast.5), custom_call_target="tpu_custom_call" | custom-call | tf_op jit(solution)/shard_map/pallas_call | solution.py:258
  54.9 2.8 %shard_map.69 = (f32[1024,256]{1,0:T(8,128)}, f32[1024,256]{1,0:T(8,128)}) custom-call(f32[1024,256]{1,0:T(8,128)} %signal_ref.1, bf16[1024,256]{1,0:T(8,128)(2,1)} %bitcast.6, bf16[1024,256]{1,0:T(8,128)(2,1)} %bitcast.7), custom_call_target="tpu_custom_call" | custom-call | tf_op jit(solution)/shard_map/pallas_call | solution.py:310

commit v7 on v6

--- a/solution.py
+++ b/solution.py
@@ -43,21 +43,23 @@
     res_proj,
     skip_proj,
     swap256,
-    split512,
     join512,
     turn512,
     enter512,
     sent_xy,
     sent_z,
-    sent_late,
+    late_sent_xy,
+    late_sent_z,
     first_xy,
     first_z,
     next_z,
     next_xy,
     halves,
-    late_first,
-    late_next,
-    late,
+    late_first_xy,
+    late_first_z,
+    late_next_z,
+    late_next_xy,
+    late_halves,
     leave,
     passing,
     last,
@@ -95,7 +97,6 @@
     for copy in weights:
         copy.start()
     swap256[...] = one_hot(256, lambda o: (o & 15) * 16 + (o >> 4))
-    split512[...] = one_hot(LENGTH, lambda o: (o & 31) * 16 + (o >> 5))
     join512[...] = one_hot(LENGTH, lambda o: (o & 15) * 32 + (o >> 4))
     turn512[...] = one_hot(LENGTH, lambda o: ((o >> 1) & 15) * 32 + (o >> 5) * 2 + (o & 1))
     enter512[...] = one_hot(
@@ -108,10 +109,11 @@
     cur[pl.ds(PAD + LENGTH, PAD), :] = jnp.zeros((PAD, C), F32)
     load.wait()
     slab = (GROUP, 16, C)
-    sent_xy[...] = signal[0, pl.ds(0, 256), :].astype(BF16).reshape(slab)
-    sent_z[...] = reordered(swap256[...], signal[1, pl.ds(0, 256), :].astype(BF16)).astype(BF16).reshape(slab)
-    for half in range(HALVES):
-        sent_late[:, half] = signal[half, pl.ds(256, 256), :].astype(BF16).reshape(slab)
+    for chunk, across, along in ((0, sent_xy, sent_z), (1, late_sent_xy, late_sent_z)):
+        at = pl.ds(chunk * 256, 256)
+        across[...] = signal[0, at, :].astype(BF16).reshape(slab)
+        rows = reordered(swap256[...], signal[1, at, :].astype(BF16))
+        along[...] = rows.astype(BF16).reshape(slab)
     for copy in weights:
         copy.wait()
     for layer in range(LAYERS):
@@ -148,19 +150,37 @@
     def wait_for(target, stage):
         finish(target, recv_sem.at[stage])
 
+    def leaves(source, stage):
+        finish(source, send_sem.at[stage])
+        del started[stage]
+
+    def turned(arrived):
+        rows = reordered(swap256[...], arrived[...].reshape(256, C))
+        return rows.astype(BF16).reshape(slab)
+
     exchange(sent_xy, first_xy, False, 0)
     exchange(sent_z, first_z, True, 1)
-    exchange(sent_late, late_first, False, 3)
+    exchange(late_sent_xy, late_first_xy, False, 3)
+    leaves(sent_z, 1)
+    exchange(late_sent_z, late_first_z, True, 14)
     wait_for(first_xy, 0)
-    next_z[...] = reordered(swap256[...], first_xy[...].reshape(256, C)).astype(BF16).reshape(slab)
+    next_z[...] = turned(first_xy)
     exchange(next_z, halves.at[0], True, 2)
     wait_for(first_z, 1)
-    next_xy[...] = reordered(swap256[...], first_z[...].reshape(256, C)).astype(BF16).reshape(slab)
+    next_xy[...] = turned(first_z)
     exchange(next_xy, halves.at[1], False, 4)
-    wait_for(late_first, 3)
-    rows = reordered(split512[...], late_first[...].reshape(LENGTH, C))
-    late_next[...] = rows.astype(BF16).reshape(GROUP, 32, C)
-    exchange(late_next, late, True, 5)
+    wait_for(late_first_xy, 3)
+    late_next_z[...] = turned(late_first_xy)
+    leaves(next_z, 2)
+    exchange(late_next_z, late_halves.at[0], True, 5)
+    wait_for(late_first_z, 14)
+    late_next_xy[...] = turned(late_first_z)
+    exchange(late_next_xy, late_halves.at[1], False, 15)
+
+    def enter(arrived):
+        rows = reordered(enter512[...], arrived[...].reshape(LENGTH, C))
+        cur[pl.ds(PAD, LENGTH), :] = rows
+        start[...] = rows.astype(BF16)
 
     def layers():
         for layer in range(LAYERS):
@@ -208,18 +228,15 @@
 
     wait_for(halves.at[0], 2)
     wait_for(halves.at[1], 4)
-    rows = reordered(enter512[...], halves[...].reshape(LENGTH, C))
-    cur[pl.ds(PAD, LENGTH), :] = rows
-    start[...] = rows.astype(BF16)
+    enter(halves)
     layers()
     leave_along_z(0, 0, 6)
     skip_sums()
     leave_along_z(1, 1, 7)
 
-    wait_for(late, 5)
-    rows = reordered(turn512[...], late[...].reshape(LENGTH, C))
-    cur[pl.ds(PAD, LENGTH), :] = rows
-    start[...] = rows.astype(BF16)
+    wait_for(late_halves.at[0], 5)
+    wait_for(late_halves.at[1], 15)
+    enter(late_halves)
     layers()
     leave[2] = result[0].reshape(wide)
     exchange(leave.at[2], passing.at[2], False, 8)
@@ -269,18 +286,20 @@
             vmem(LENGTH, LENGTH),
             vmem(LENGTH, LENGTH),
             vmem(LENGTH, LENGTH),
-            vmem(LENGTH, LENGTH),
-            vmem(GROUP, 16, C),
-            vmem(GROUP, 16, C),
-            vmem(GROUP, HALVES, 16, C),
+            vmem(GROUP, 16, C),
+            vmem(GROUP, 16, C),
+            vmem(GROUP, 16, C),
+            vmem(GROUP, 16, C),
             vmem(GROUP, 16, C),
             vmem(GROUP, 16, C),
             vmem(GROUP, 16, C),
             vmem(GROUP, 16, C),
             vmem(2, GROUP, 16, C),
-            vmem(GROUP, HALVES, 16, C),
-            vmem(GROUP, 32, C),
-            vmem(GROUP, 32, C),
+            vmem(GROUP, 16, C),
+            vmem(GROUP, 16, C),
+            vmem(GROUP, 16, C),
+            vmem(GROUP, 16, C),
+            vmem(2, GROUP, 16, C),
             vmem(4, GROUP, 32, C),
             vmem(4, GROUP, 32, C),
             vmem(4, GROUP, HALVES, 16, C),
@@ -291,8 +310,8 @@
             vmem(LENGTH, 3 * C),
             pltpu.SemaphoreType.DMA,
             pltpu.SemaphoreType.DMA((3,)),
-            pltpu.SemaphoreType.DMA((14,)),
-            pltpu.SemaphoreType.DMA((14,)),
+            pltpu.SemaphoreType.DMA((16,)),
+            pltpu.SemaphoreType.DMA((16,)),
             pltpu.SemaphoreType.DMA((4,)),
         ],
         compiler_params=pltpu.CompilerParams(

time: 57.8 us -> 58.1 us (level)
  no operation moved by 1% of the time
where the time goes in v7:
time: 58.1 us; the launch traced here: 57.9 us
  Pallas kernels  57.3 us (99%)
  between operations  0.64 us (1%)
    pallas_call x1, Pallas kernels, body(): pl.pallas_call(kernel, out_shape=[jax.ShapeDtypeStruct((HALVES, RESIDUES,...  54.5 us
    pallas_call x1, Pallas kernels, body(): pl.pallas_call(finish_kernel, grid=(HALVES,), out_shape=[jax.ShapeDtypeSt...  2.76 us

profile of v7, /device:TPU:1, one launch (start us, length us, event | category | flops | bytes accessed | tf_op | source)
XLA Modules:
  0.0 57.9 jit_solution(1524070337250813348)
XLA Ops:
  0.6 54.5 %shard_map.68 = (bf16[2,512,256]{2,1,0:T(8,128)(2,1)}, bf16[2,512,256]{2,1,0:T(8,128)(2,1)}) custom-call(f32[2,512,256]{2,1,0:T(8,128)} %bitcast.4, bf16[6,768,512]{2,1,0:T(8,128)(2,1)} %conv_hbm.1, f32[6,512]{1,0:T(8,128)} %bias_ref.1, bf16[6,256,256]{2,1,0:T(8,128)(2,1)} %res_hbm.1, bf16[1536,256]{1,0:T(8,128)(2,1)} %bitcast.5), custom_call_target="tpu_custom_call" | custom-call | tf_op jit(solution)/shard_map/pallas_call | solution.py:275
  55.2 2.8 %shard_map.69 = (f32[1024,256]{1,0:T(8,128)}, f32[1024,256]{1,0:T(8,128)}) custom-call(f32[1024,256]{1,0:T(8,128)} %signal_ref.1, bf16[1024,256]{1,0:T(8,128)(2,1)} %bitcast.6, bf16[1024,256]{1,0:T(8,128)(2,1)} %bitcast.7), custom_call_target="tpu_custom_call" | custom-call | tf_op jit(solution)/shard_map/pallas_call | solution.py:329

commit v8 on v6

--- a/solution.py
+++ b/solution.py
@@ -33,13 +33,14 @@
 def kernel(
     signal_hbm,
     conv_hbm,
-    bias_ref,
+    bias_hbm,
     res_hbm,
     skip_hbm,
     delta_out,
     skip_out,
     signal,
     conv,
+    bias_ref,
     res_proj,
     skip_proj,
     swap256,
@@ -91,6 +92,7 @@
         pltpu.make_async_copy(conv_hbm, conv, weight_sem.at[0]),
         pltpu.make_async_copy(res_hbm, res_proj, weight_sem.at[1]),
         pltpu.make_async_copy(skip_hbm, skip_proj, weight_sem.at[2]),
+        pltpu.make_async_copy(bias_hbm, bias_ref, weight_sem.at[3]),
     ]
     for copy in weights:
         copy.start()
@@ -258,11 +260,12 @@
     delta, skip_sum = pl.pallas_call(
         kernel,
         out_shape=[jax.ShapeDtypeStruct((HALVES, RESIDUES, C), BF16)] * 2,
-        in_specs=[any_space, any_space, pl.BlockSpec(memory_space=pltpu.VMEM), any_space, any_space],
+        in_specs=[any_space] * 5,
         out_specs=[any_space, any_space],
         scratch_shapes=[
             vmem(HALVES, RESIDUES, C, dtype=F32),
             vmem(LAYERS, 3 * C, 2 * C),
+            vmem(LAYERS, 2 * C, dtype=F32),
             vmem(LAYERS, C, C),
             vmem(LAYERS * C, C),
             vmem(256, 256),
@@ -290,7 +293,7 @@
             vmem(2, LENGTH, C),
             vmem(LENGTH, 3 * C),
             pltpu.SemaphoreType.DMA,
-            pltpu.SemaphoreType.DMA((3,)),
+            pltpu.SemaphoreType.DMA((4,)),
             pltpu.SemaphoreType.DMA((14,)),
             pltpu.SemaphoreType.DMA((14,)),
             pltpu.SemaphoreType.DMA((4,)),

time: 57.8 us -> 57.5 us (level)
  no operation moved by 1% of the time
where the time goes in v8:
time: 57.5 us; the launch traced here: 57.4 us
  Pallas kernels  56.7 us (99%)
  between operations  0.64 us (1%)
    pallas_call x1, Pallas kernels, body(): pl.pallas_call(kernel, out_shape=[jax.ShapeDtypeStruct((HALVES, RESIDUES,...  54 us
    pallas_call x1, Pallas kernels, body(): pl.pallas_call(finish_kernel, grid=(HALVES,), out_shape=[jax.ShapeDtypeSt...  2.75 us

profile of v8, /device:TPU:1, one launch (start us, length us, event | category | flops | bytes accessed | tf_op | source)
XLA Modules:
  0.0 57.4 jit_solution(5373446167389156435)
XLA Ops:
  0.6 54.0 %shard_map.68 = (bf16[2,512,256]{2,1,0:T(8,128)(2,1)}, bf16[2,512,256]{2,1,0:T(8,128)(2,1)}) custom-call(f32[2,512,256]{2,1,0:T(8,128)} %bitcast.4, bf16[6,768,512]{2,1,0:T(8,128)(2,1)} %conv_hbm.1, f32[6,512]{1,0:T(8,128)} %bias_hbm.1, bf16[6,256,256]{2,1,0:T(8,128)(2,1)} %res_hbm.1, bf16[1536,256]{1,0:T(8,128)(2,1)} %bitcast.5), custom_call_target="tpu_custom_call" | custom-call | tf_op jit(solution)/shard_map/pallas_call | solution.py:260
  54.6 2.8 %shard_map.69 = (f32[1024,256]{1,0:T(8,128)}, f32[1024,256]{1,0:T(8,128)}) custom-call(f32[1024,256]{1,0:T(8,128)} %signal_ref.1, bf16[1024,256]{1,0:T(8,128)(2,1)} %bitcast.6, bf16[1024,256]{1,0:T(8,128)(2,1)} %bitcast.7), custom_call_target="tpu_custom_call" | custom-call | tf_op jit(solution)/shard_map/pallas_call | solution.py:313

commit v9 on v8

--- a/solution.py
+++ b/solution.py
@@ -97,15 +97,6 @@
     for copy in weights:
         copy.start()
     swap256[...] = one_hot(256, lambda o: (o & 15) * 16 + (o >> 4))
-    split512[...] = one_hot(LENGTH, lambda o: (o & 31) * 16 + (o >> 5))
-    join512[...] = one_hot(LENGTH, lambda o: (o & 15) * 32 + (o >> 4))
-    turn512[...] = one_hot(LENGTH, lambda o: ((o >> 1) & 15) * 32 + (o >> 5) * 2 + (o & 1))
-    enter512[...] = one_hot(
-        LENGTH,
-        lambda o: jnp.where(
-            (o & 1) == 0, ((o >> 1) & 15) * 16 + (o >> 5), 256 + (o >> 5) * 16 + ((o >> 1) & 15)
-        ),
-    )
     cur[pl.ds(0, PAD), :] = jnp.zeros((PAD, C), F32)
     cur[pl.ds(PAD + LENGTH, PAD), :] = jnp.zeros((PAD, C), F32)
     load.wait()
@@ -114,13 +105,6 @@
     sent_z[...] = reordered(swap256[...], signal[1, pl.ds(0, 256), :].astype(BF16)).astype(BF16).reshape(slab)
     for half in range(HALVES):
         sent_late[:, half] = signal[half, pl.ds(256, 256), :].astype(BF16).reshape(slab)
-    for copy in weights:
-        copy.wait()
-    for layer in range(LAYERS):
-        conv[layer, :, pl.ds(C, C)] = conv[layer, :, pl.ds(C, C)] * jnp.asarray(0.5, BF16)
-        res_proj[layer] = res_proj[layer] * jnp.asarray(0.5, BF16)
-        at = pl.ds(layer * C, C)
-        skip_proj[at, :] = skip_proj[at, :] * jnp.asarray(0.5, BF16)
     pl.semaphore_wait(barrier, 2 * (GROUP - 1))
 
     started = {}
@@ -153,6 +137,22 @@
     exchange(sent_xy, first_xy, False, 0)
     exchange(sent_z, first_z, True, 1)
     exchange(sent_late, late_first, False, 3)
+    split512[...] = one_hot(LENGTH, lambda o: (o & 31) * 16 + (o >> 5))
+    join512[...] = one_hot(LENGTH, lambda o: (o & 15) * 32 + (o >> 4))
+    turn512[...] = one_hot(LENGTH, lambda o: ((o >> 1) & 15) * 32 + (o >> 5) * 2 + (o & 1))
+    enter512[...] = one_hot(
+        LENGTH,
+        lambda o: jnp.where(
+            (o & 1) == 0, ((o >> 1) & 15) * 16 + (o >> 5), 256 + (o >> 5) * 16 + ((o >> 1) & 15)
+        ),
+    )
+    for copy in weights:
+        copy.wait()
+    for layer in range(LAYERS):
+        conv[layer, :, pl.ds(C, C)] = conv[layer, :, pl.ds(C, C)] * jnp.asarray(0.5, BF16)
+        res_proj[layer] = res_proj[layer] * jnp.asarray(0.5, BF16)
+        at = pl.ds(layer * C, C)
+        skip_proj[at, :] = skip_proj[at, :] * jnp.asarray(0.5, BF16)
     wait_for(first_xy, 0)
     next_z[...] = reordered(swap256[...], first_xy[...].reshape(256, C)).astype(BF16).reshape(slab)
     exchange(next_z, halves.at[0], True, 2)

time: 57.5 us -> 56.9 us (0.990)
  Pallas kernels: 56.7 us -> 56.1 us
    pallas_call x1, Pallas kernels: 54 us -> 53.4 us  [body(): pl.pallas_call(kernel, out_shape=[jax.ShapeDtypeStruct((HALVES, RESIDUES,...]
where the time goes in v9:
time: 56.9 us; the launch traced here: 56.8 us
  Pallas kernels  56.1 us (99%)
  between operations  0.64 us (1%)
    pallas_call x1, Pallas kernels, body(): pl.pallas_call(kernel, out_shape=[jax.ShapeDtypeStruct((HALVES, RESIDUES,...  53.4 us
    pallas_call x1, Pallas kernels, body(): pl.pallas_call(finish_kernel, grid=(HALVES,), out_shape=[jax.ShapeDtypeSt...  2.75 us

profile of v9, /device:TPU:1, one launch (start us, length us, event | category | flops | bytes accessed | tf_op | source)
XLA Modules:
  0.0 56.8 jit_solution(17570002178965634975)
XLA Ops:
  0.6 53.4 %shard_map.68 = (bf16[2,512,256]{2,1,0:T(8,128)(2,1)}, bf16[2,512,256]{2,1,0:T(8,128)(2,1)}) custom-call(f32[2,512,256]{2,1,0:T(8,128)} %bitcast.4, bf16[6,768,512]{2,1,0:T(8,128)(2,1)} %conv_hbm.1, f32[6,512]{1,0:T(8,128)} %bias_hbm.1, bf16[6,256,256]{2,1,0:T(8,128)(2,1)} %res_hbm.1, bf16[1536,256]{1,0:T(8,128)(2,1)} %bitcast.5), custom_call_target="tpu_custom_call" | custom-call | tf_op jit(solution)/shard_map/pallas_call | solution.py:260
  54.0 2.8 %shard_map.69 = (f32[1024,256]{1,0:T(8,128)}, f32[1024,256]{1,0:T(8,128)}) custom-call(f32[1024,256]{1,0:T(8,128)} %signal_ref.1, bf16[1024,256]{1,0:T(8,128)(2,1)} %bitcast.6, bf16[1024,256]{1,0:T(8,128)(2,1)} %bitcast.7), custom_call_target="tpu_custom_call" | custom-call | tf_op jit(solution)/shard_map/pallas_call | solution.py:313
